TPU v7x, 512 devices: a whole 4x4x16 slice. The times are simulated.
512 devices in a mesh: section: 8 (over x_hi, y), tp: 64 (over x_lo, z, core).
Axes of the slice: x: 4 (x_hi: 2, x_lo: 2; x = x_hi * 2 + x_lo), y: 4, z: 16, core: 2. Of those that a mesh axis runs over, the one named last changes fastest.
Arguments:
- resid: bfloat16 [8, 16, 8192], P('section', None, 'tp'), may hold values from -6 to 6
- norm_gain: bfloat16 [8, 8192], P('section'), may hold values from 0.5 to 1.5
- query_weight: bfloat16 [8, 8192, 8192], P('section', None, 'tp'), may hold values from -0.0625 to 0.0625
- key_value_weight: bfloat16 [8, 8192, 2048], P('section', None, 'tp'), may hold values from -0.0625 to 0.0625
- out_weight: bfloat16 [8, 8192, 8192], P('section', None, 'tp'), may hold values from -0.25 to 0.25
- key_value_cache: bfloat16 [8, 16, 384, 2048], P('section', None, 'tp'), may hold values from -51 to 51
- lengths: int32 [8, 16], P('section'), may hold values from 1 to 384, as said below
- positions: int32 [8, 16], P('section'), may hold values from 1 to 8575, as said below
Outputs:
- next_input: bfloat16 [8, 16, 8192], P('section', None, 'tp')
Inputs may be any that keep to these rules, and one draw needn't show every extreme that they name: `lengths`: at most 384; in every section some row has exactly 384. `positions`: each row's position is at least its length and at most its length + 8191; in every section some row has exactly 8575.
All inputs are finite; a program needn't handle non-finite values.
Results may differ from a plain program's by a relative error of at most 0.012.
The roundings to bfloat16 on the way count: a program that leaves them out, or rounds other values in their place, can miss the bound.
Values may be sent and summed in bfloat16 or wider, within the bound.
No kernel may reach another device: no remote copies, remote signals or barrier semaphores. Data moves between devices by JAX's collectives and lax.ppermute only.
A program may use at most 192 MiB of HBM per device.

v0:
```python
import math

import jax
import jax.numpy as jnp
from jax import lax
from jax.sharding import PartitionSpec as P

HEAD_WIDTH = 128
KEY_VALUE_HEADS = 8


def combined_all(value, axis, join):
    pieces = jax.tree.map(lambda part: lax.all_gather(part, axis), value)
    head = jax.tree.map(lambda part: part[0], pieces)
    tail = jax.tree.map(lambda part: part[1:], pieces)
    running, _ = lax.scan(lambda running, share: (join(running, share), None), head, tail)
    return running


def from_behind(array, axis, by):
    devices = lax.axis_size(axis)
    return lax.ppermute(array, axis, [(i, (i + by) % devices) for i in range(devices)])


def apply_rotary(vectors, token_positions):
    half_size = vectors.shape[-1] // 2
    freqs = jnp.exp(
        -math.log(500000.0) * 2.0 * jnp.arange(half_size, dtype=jnp.float32) / vectors.shape[-1]
    )
    angles = token_positions.astype(jnp.float32)[:, None, None] * freqs
    cosine = jnp.cos(angles)
    sine = jnp.sin(angles)
    first = vectors[..., :half_size]
    second = vectors[..., half_size:]
    return jnp.concatenate(
        [first * cosine - second * sine, second * cosine + first * sine], axis=-1
    )


def join(earlier, later):
    peak_one, total_one, mix_one = earlier
    peak_two, total_two, mix_two = later
    peak_score = jnp.maximum(peak_one, peak_two)
    scale_one = jnp.exp(peak_one - peak_score)
    scale_two = jnp.exp(peak_two - peak_score)
    totals = total_one * scale_one + total_two * scale_two
    mixture = mix_one * scale_one[..., None] + mix_two * scale_two[..., None]
    return (peak_score, totals, mixture)


def body(
    resid,
    norm_gain,
    query_weight,
    key_value_weight,
    out_weight,
    key_value_cache,
    lengths,
    positions,
):
    count_rows = resid.shape[1]
    gathered = lax.all_gather(resid, "tp", axis=2, tiled=True)[0]
    widened = gathered.astype(jnp.float32)
    meansq = jnp.mean(widened * widened, axis=-1, keepdims=True)
    normed = (widened * lax.rsqrt(meansq + 1e-05) * norm_gain[0].astype(jnp.float32)).astype(
        jnp.bfloat16
    )
    token_positions = positions[0]
    own_heads = query_weight.shape[2] // HEAD_WIDTH
    query_own = jnp.dot(normed, query_weight[0], preferred_element_type=jnp.float32).reshape(
        count_rows, own_heads, HEAD_WIDTH
    )
    query_own = (
        apply_rotary(query_own, token_positions)
        .astype(jnp.bfloat16)
        .reshape(count_rows, own_heads * HEAD_WIDTH)
    )
    keyval_own = jnp.dot(normed, key_value_weight[0], preferred_element_type=jnp.float32).astype(
        jnp.bfloat16
    )
    query_full, key_value_full = (
        lax.all_gather(query_own, "tp", axis=1, tiled=True),
        lax.all_gather(keyval_own, "tp", axis=1, tiled=True),
    )
    number_heads = query_full.shape[1] // HEAD_WIDTH
    queries_per_group = number_heads // KEY_VALUE_HEADS
    fresh_key = apply_rotary(
        key_value_full[:, : KEY_VALUE_HEADS * HEAD_WIDTH]
        .reshape(count_rows, KEY_VALUE_HEADS, HEAD_WIDTH)
        .astype(jnp.float32),
        token_positions,
    ).astype(jnp.bfloat16)
    fresh_value = (
        key_value_full[:, KEY_VALUE_HEADS * HEAD_WIDTH :]
        .reshape(count_rows, KEY_VALUE_HEADS, HEAD_WIDTH)
        .astype(jnp.float32)
    )
    cache_piece = key_value_cache[0]
    span_length = cache_piece.shape[1]
    first_slot = lax.axis_index("tp") * span_length
    stored_keys = (
        cache_piece[:, :, : KEY_VALUE_HEADS * HEAD_WIDTH]
        .reshape(count_rows, span_length, KEY_VALUE_HEADS, HEAD_WIDTH)
        .astype(jnp.float32)
    )
    stored_values = (
        cache_piece[:, :, KEY_VALUE_HEADS * HEAD_WIDTH :]
        .reshape(count_rows, span_length, KEY_VALUE_HEADS, HEAD_WIDTH)
        .astype(jnp.float32)
    )
    query_groups = query_full.astype(jnp.float32).reshape(
        count_rows, KEY_VALUE_HEADS, queries_per_group, HEAD_WIDTH
    )
    factor = 1.0 / math.sqrt(HEAD_WIDTH)
    scores = jnp.einsum("rkgd,rtkd->rkgt", query_groups, stored_keys) * factor
    slot_index = first_slot + jnp.arange(span_length, dtype=jnp.int32)
    live_mask = (slot_index[None, :] < lengths[0][:, None])[:, None, None, :]
    local_peak = jnp.max(jnp.where(live_mask, scores, -1e30), axis=-1)
    weights = jnp.where(live_mask, jnp.exp(scores - local_peak[..., None]), 0.0)
    local_total = jnp.sum(weights, axis=-1).reshape(count_rows, number_heads)
    local_mix = jnp.einsum("rkgt,rtkd->rkgd", weights, stored_values).reshape(
        count_rows, number_heads, HEAD_WIDTH
    )
    local_peak = local_peak.reshape(count_rows, number_heads)
    new_score = (
        jnp.einsum("rkgd,rkd->rkg", query_groups, fresh_key.astype(jnp.float32)) * factor
    ).reshape(count_rows, number_heads)
    value_heads = jnp.broadcast_to(
        fresh_value[:, :, None, :], (count_rows, KEY_VALUE_HEADS, queries_per_group, HEAD_WIDTH)
    ).reshape(count_rows, number_heads, HEAD_WIDTH)
    merged = combined_all((local_peak, local_total, local_mix), "tp", join)
    peak_score, totals, mixture = join(merged, (new_score, jnp.ones_like(new_score), value_heads))
    attn = (
        (mixture / totals[..., None])
        .astype(jnp.bfloat16)
        .reshape(count_rows, number_heads * HEAD_WIDTH)
    )
    projected = jnp.dot(attn, out_weight[0], preferred_element_type=jnp.float32)
    updated = (resid[0].astype(jnp.float32) + projected).astype(jnp.bfloat16)
    return from_behind(updated, "section", 1)[None]


def solution(mesh):
    return jax.shard_map(
        body,
        mesh=mesh,
        in_specs=(
            P("section", None, "tp"),
            P("section", None),
            P("section", None, "tp"),
            P("section", None, "tp"),
            P("section", None, "tp"),
            P("section", None, "tp", None),
            P("section", None),
            P("section", None),
        ),
        out_specs=P("section", None, "tp"),
        check_vma=False,
    )
```

profile of v0, /device:TPU:1, one launch (start us, length us, event | category | flops | bytes accessed | tf_op | source)
XLA Modules:
  0.0 479.8 jit_solution(8716863634988787162)
XLA Ops:
  8.2 71.9 %all_gather.18 = bf16[1,16,8192]{2,1,0:T(8,128)(2,1)S(1)} all-gather(bf16[1,16,128]{2,1,0:T(8,128)(2,1)} %param.10), channel_id=1, replica_groups=mesh['section'=8,'tp'=64] {'tp'}, dimensions={2}, use_global_device_ids=true | all-gather | bytes 266240 | tf_op jit(solution)/shard_map/all_gather | solution.py:62
  81.0 60.2 %all_gather.19 = bf16[16,8192]{1,0:T(8,128)(2,1)S(1)} all-gather(bf16[16,128]{1,0:T(8,128)(2,1)S(1)} %pad_maximum_fusion), channel_id=1, replica_groups=mesh['section'=8,'tp'=64] {'tp'}, dimensions={1}, use_global_device_ids=true | all-gather | bytes 266240 | tf_op jit(solution)/shard_map/all_gather | solution.py:82
  143.6 63.0 %all-gather = bf16[64,32,16]{1,2,0:T(8,128)(2,1)S(1)} all-gather(bf16[1,32,16]{1,2,0:T(8,128)(2,1)S(1)} %fusion.16), channel_id=1, replica_groups=mesh['section'=8,'tp'=64] {'tp'}, dimensions={0}, use_global_device_ids=true | all-gather | bytes 66560 | tf_op jit(solution)/shard_map/all_gather | solution.py:83
  208.3 62.6 %all_gather.21 = f32[64,16,64]{2,1,0:T(8,128)S(1)} all-gather(f32[1,16,64]{2,1,0:T(8,128)S(1)} %copy.43), channel_id=1, replica_groups=mesh['section'=8,'tp'=64] {'tp'}, dimensions={0}, use_global_device_ids=true | all-gather | bytes 266240 | tf_op jit(solution)/shard_map/all_gather | solution.py:13
  270.9 64.0 %all_gather.20 = f32[64,16,64]{2,1,0:T(8,128)S(1)} all-gather(f32[1,16,64]{2,1,0:T(8,128)S(1)} %copy.41), channel_id=1, replica_groups=mesh['section'=8,'tp'=64] {'tp'}, dimensions={0}, use_global_device_ids=true | all-gather | bytes 266240 | tf_op jit(solution)/shard_map/all_gather | solution.py:13
  334.9 2.0 all-gather.3.cloned.1.call-done
  338.0 23.3 %slice.65 = f32[63,16,64,128]{3,2,1,0:T(8,128)} slice(f32[64,16,64,128]{3,2,1,0:T(8,128)} %all-gather.3.cloned.1.call-done), slice={[1:64], [0:16], [0:64], [0:128]} | slice | bytes 66060288 | tf_op jit(solution)/shard_map/slice | solution.py:15
  361.4 100.3 %while.14 = (s32[]{:T(128)}, f32[16,64]{1,0:T(8,128)S(1)}, f32[16,64]{1,0:T(8,128)S(1)}, f32[16,64,128]{2,1,0:T(8,128)S(1)}, f32[63,16,64]{2,1,0:T(8,128)S(1)}, ...) while((s32[]{:T(128)}, f32[16,64]{1,0:T(8,128)S(1)}, f32[16,64]{1,0:T(8,128)S(1)}, ...), condition=%wide.region_4.5_spmd, body=%wide.region_3.4_spmd.sunk | while | flops 399362 | bytes 1613925 | solution.py:16
  361.4 1.5 fusion.60
  363.0 1.5 fusion.60
  364.6 1.5 fusion.60
  366.2 1.5 fusion.60
  367.8 1.5 fusion.60
  369.4 1.5 fusion.60
  370.9 1.5 fusion.60
  372.5 1.5 fusion.60
  374.1 1.5 fusion.60
  375.7 1.5 fusion.60
  377.3 1.5 fusion.60
  407.6 1.5 fusion.60
  437.8 1.5 fusion.60
  462.2 2.2 fusion.13
  464.4 3.1 collective-permute-start
  467.5 4.8 %collective-permute-done = bf16[16,128]{1,0:T(8,128)(2,1)S(1)} collective-permute-done((bf16[16,128]{1,0:T(8,128)(2,1)S(1)}, bf16[16,128]{1,0:T(8,128)(2,1)S(1)}, u32[]{:S(2)}, u32[]{:S(2)}) %collective-permute-start) | collective-permute-done | bytes 4128 | tf_op jit(solution)/shard_map/ppermute | solution.py:22
  (169 shorter events, 87.2 us)
Async XLA Ops:
  6.5 73.8 %copy-start = (bf16[1,8192,128]{2,1,0:T(8,128)(2,1)S(1)}, bf16[1,8192,128]{2,1,0:T(8,128)(2,1)}, u32[]{:S(2)}) copy-start(bf16[1,8192,128]{2,1,0:T(8,128)(2,1)} %param.12) | copy-start | bytes 6291460
  6.5 134.7 %copy-start.3 = (bf16[1,16,6,2048]{3,1,2,0:T(8,128)(2,1)S(1)}, bf16[1,16,6,2048]{3,1,2,0:T(8,128)(2,1)}, u32[]{:S(2)}) copy-start(bf16[1,16,6,2048]{3,1,2,0:T(8,128)(2,1)} %param.15) | copy-start | bytes 1179652
  6.5 330.4 %all-gather.3.cloned.1.call-start = ((), (), s32[]{:S(2)}) async-start(), calls=%async_computation | async-start | bytes 34078720 | tf_op jit(solution)/shard_map/all_gather | solution.py:13
  80.3 61.1 %copy-start.5 = (s32[1,16]{1,0:T(1,128)S(1)}, s32[1,16]{1,0:T(1,128)}, u32[]{:S(2)}) copy-start(s32[1,16]{1,0:T(1,128)} %param.16) | copy-start | bytes 196
  141.3 2.0 copy-start.2
  361.4 100.8 %copy-start.4 = (bf16[1,16,128]{2,1,0:T(8,128)(2,1)S(1)}, bf16[1,16,128]{2,1,0:T(8,128)(2,1)}, u32[]{:S(2)}) copy-start(bf16[1,16,128]{2,1,0:T(8,128)(2,1)} %param.10) | copy-start | bytes 12292
  461.7 11.3 %copy-start.1 = (bf16[1,8192,128]{2,1,0:T(8,128)(2,1)S(1)}, bf16[1,8192,128]{2,1,0:T(8,128)(2,1)}, u32[]{:S(2)}) copy-start(bf16[1,8192,128]{2,1,0:T(8,128)(2,1)} %param.12) | copy-start | bytes 6291460
  464.4 8.0 %collective-permute-start = (bf16[16,128]{1,0:T(8,128)(2,1)S(1)}, bf16[16,128]{1,0:T(8,128)(2,1)S(1)}, u32[]{:S(2)}, u32[]{:S(2)}) collective-permute-start(bf16[16,128]{1,0:T(8,128)(2,1)S(1)} %fusion.13), channel_id=1, source_target_pairs={{0,64},{64,128},{128,192},{192,256},{256,320},{320,384},{384,448},... | collective-permute-start | bytes 12296 | tf_op jit(solution)/shard_map/ppermute | solution.py:22
Sparse Core Ops, SparseCore 0:
  143.3 193.5 all-gather.2
where the time goes:
time: 483 us; the launch traced here: 480 us
  blocking collectives  322 us (67%)
  other arithmetic  102 us (21%)
  local copies, waits for them, and re-layouts  26.1 us (5%)
  between operations  13.6 us (3%)
  waiting for transfers between devices  6.89 us (1%)
  matrix products  4.91 us (1%)
    all_gather x2, blocking collectives, combined_all(): pieces = jax.tree.map(lambda part: lax.all_gather(part, axis), value)  127 us
    add x63, other arithmetic, join(): mixture = mix_one * scale_one[..., None] + mix_two * scale_two[..., None]  97.6 us
    all_gather x1, blocking collectives, body(): gathered = lax.all_gather(resid, 'tp', axis=2, tiled=True)[0]  71.9 us
    all_gather x1, blocking collectives, body(): lax.all_gather(keyval_own, 'tp', axis=1, tiled=True)  63 us
    all_gather x1, blocking collectives, body(): lax.all_gather(query_own, 'tp', axis=1, tiled=True)  60.2 us
    slice x3, local copies, waits for them, and re-layouts, combined_all(): tail = jax.tree.map(lambda part: part[1:], pieces)  23.4 us
  transfers between devices with their start and end apart: 2, of which 2 were waited for; matrix products, arithmetic and copies ran while one was open for 0% of the time, Pallas kernels for 0%

commit v1 on v0

v1 whole, which is shorter than its diff:
```python
import math

import jax
import jax.numpy as jnp
from jax import lax
from jax.sharding import Mesh
from jax.sharding import PartitionSpec as P

HEAD_WIDTH = 128
KEY_VALUE_HEADS = 8
MINOR = ("x", "z", "c")


def rotary_tables(token_positions):
    half_size = HEAD_WIDTH // 2
    freqs = jnp.exp(
        -math.log(500000.0) * 2.0 * jnp.arange(half_size, dtype=jnp.float32) / HEAD_WIDTH
    )
    angles = token_positions.astype(jnp.float32)[:, None] * freqs
    return jnp.cos(angles), jnp.sin(angles)


def rotate(vectors, cosine, sine):
    half_size = vectors.shape[-1] // 2
    first = vectors[..., :half_size]
    second = vectors[..., half_size:]
    return jnp.concatenate(
        [first * cosine - second * sine, second * cosine + first * sine], axis=-1
    )


def spread(part):
    line = lax.axis_size("z")
    copies = jnp.broadcast_to(part[None], (line,) + part.shape)
    along = lax.all_to_all(copies, "z", 0, 0)
    full = lax.all_gather(along, ("x", "c"))
    return full.reshape((lax.axis_size("x"), lax.axis_size("c"), line) + part.shape)


def body(
    resid,
    norm_gain,
    query_weight,
    key_value_weight,
    out_weight,
    key_value_cache,
    lengths,
    positions,
):
    rows = resid.shape[1]
    devices = lax.axis_size("x") * lax.axis_size("z") * lax.axis_size("c")
    groups = KEY_VALUE_HEADS
    members = devices // groups
    own_rows = rows // members
    me = lax.axis_index(MINOR)
    group, member = me // members, me % members
    span = key_value_cache.shape[2]

    pieces = key_value_cache[0].reshape(members, own_rows, span, 2, groups, HEAD_WIDTH)
    pieces = pieces.transpose(4, 0, 3, 2, 1, 5).reshape(
        devices, 2 * span * own_rows, HEAD_WIDTH
    )
    stored = lax.all_to_all(pieces, MINOR, 0, 0)

    gathered = spread(resid[0])
    widened = gathered.transpose(3, 0, 2, 1, 4).reshape(rows, -1).astype(jnp.float32)
    meansq = jnp.mean(widened * widened, axis=-1, keepdims=True)
    normed = (widened * lax.rsqrt(meansq + 1e-05) * norm_gain[0].astype(jnp.float32)).astype(
        jnp.bfloat16
    )
    cosine, sine = rotary_tables(positions[0])
    query = rotate(
        jnp.dot(normed, query_weight[0], preferred_element_type=jnp.float32), cosine, sine
    ).astype(jnp.bfloat16)
    keyval = jnp.dot(normed, key_value_weight[0], preferred_element_type=jnp.float32).astype(
        jnp.bfloat16
    )
    width = keyval.shape[1]
    shares = HEAD_WIDTH // width
    lane_share = jnp.arange(HEAD_WIDTH, dtype=jnp.int32) // width
    keyval = jnp.where(
        lane_share[None, :] == me % shares, jnp.tile(keyval, (1, shares)), jnp.bfloat16(0)
    )
    own = jnp.stack(
        [
            query.reshape(members, own_rows, HEAD_WIDTH),
            keyval.reshape(members, own_rows, HEAD_WIDTH),
        ],
        axis=1,
    )
    sent = jnp.broadcast_to(own[None], (groups,) + own.shape).reshape(
        (devices,) + own.shape[1:]
    )
    fresh = lax.all_to_all(sent, MINOR, 0, 0)
    queries = lax.dynamic_slice_in_dim(fresh[:, 0], group * members, members)
    fresh_key = lax.dynamic_slice_in_dim(fresh[:, 1], group * shares, shares)
    fresh_value = lax.dynamic_slice_in_dim(
        fresh[:, 1], devices // 2 + group * shares, shares
    )
    fresh_key = fresh_key.astype(jnp.float32).sum(0)
    fresh_value = fresh_value.astype(jnp.float32).sum(0)
    own_cosine = lax.dynamic_slice_in_dim(cosine, member * own_rows, own_rows)
    own_sine = lax.dynamic_slice_in_dim(sine, member * own_rows, own_rows)
    fresh_key = rotate(fresh_key, own_cosine, own_sine).astype(jnp.bfloat16)

    own_lengths = lax.dynamic_slice_in_dim(lengths[0], member * own_rows, own_rows)
    entries = devices * 2 * span * own_rows
    entry = jnp.arange(entries, dtype=jnp.int32)
    entry_row = entry % own_rows
    entry_slot = entry // (2 * span * own_rows) * span + entry // own_rows % span
    is_key = entry // (span * own_rows) % 2 == 0
    row_index = jnp.arange(own_rows, dtype=jnp.int32)[:, None]
    live = (is_key & (entry_row == row_index)) & (entry_slot < own_lengths[:, None])
    flat = stored.reshape(entries, HEAD_WIDTH)
    factor = 1.0 / math.sqrt(HEAD_WIDTH)
    scores = (
        lax.dot_general(
            queries, flat, (((2,), (1,)), ((), ())), preferred_element_type=jnp.float32
        )
        * factor
    )
    new_score = (queries.astype(jnp.float32) * fresh_key.astype(jnp.float32)).sum(-1) * factor
    scores = jnp.where(live, scores, -1e30)
    peak = jnp.maximum(scores.max(-1), new_score)
    weights = jnp.exp(scores - peak[..., None])
    new_weight = jnp.exp(new_score - peak)
    totals = weights.sum(-1) + new_weight
    mixture = lax.dot_general(
        jnp.roll(weights.astype(jnp.bfloat16), span * own_rows, axis=-1),
        flat,
        (((2,), (0,)), ((), ())),
        preferred_element_type=jnp.float32,
    )
    mixture = mixture + new_weight[..., None] * fresh_value
    attn = (mixture / totals[..., None]).astype(jnp.bfloat16)

    full = spread(attn.reshape(members * own_rows, HEAD_WIDTH))
    x, c, line = full.shape[:3]
    inner = members // c
    full = full.reshape(x, c, line // inner, inner, members, own_rows, HEAD_WIDTH)
    full = full.transpose(3, 1, 5, 0, 2, 4, 6).reshape(rows, -1)
    projected = jnp.dot(full, out_weight[0], preferred_element_type=jnp.float32)
    updated = (resid[0].astype(jnp.float32) + projected).astype(jnp.bfloat16)
    sections = lax.axis_size("section")
    following = [(i, (i + 1) % sections) for i in range(sections)]
    return lax.ppermute(updated, "section", following)[None]


def solution(mesh):
    sections, devices = mesh.devices.shape
    chips = devices // 4
    split = Mesh(
        mesh.devices.reshape(sections, 2, chips, 2), ("section",) + MINOR
    )
    return jax.shard_map(
        body,
        mesh=split,
        in_specs=(
            P("section", None, MINOR),
            P("section", None),
            P("section", None, MINOR),
            P("section", None, MINOR),
            P("section", None, MINOR),
            P("section", None, MINOR, None),
            P("section", None),
            P("section", None),
        ),
        out_specs=P("section", None, MINOR),
        check_vma=False,
    )
```

time: 483 us -> 125 us (0.26)
  blocking collectives: 322 us -> 30.4 us
  other arithmetic: 102 us -> 2.62 us
  waiting for transfers between devices: 6.89 us -> 55 us
  starting transfers between devices: 3.12 us -> 28 us
  local copies, waits for them, and re-layouts: 26.1 us -> 4.83 us
  between operations: 13.6 us -> 0.29 us
    all_gather x5 -> x2, blocking collectives: 322 us -> 15.5 us  [spread(): full = lax.all_gather(along, ('x', 'c'))]
    add x128 -> x1, other arithmetic: 98.7 us -> 0.01 us  [body(): totals = weights.sum(-1) + new_weight]
    all_to_all x0 -> x3, waiting for transfers between devices: none -> 50.3 us  [the longest x1 26.8 us: body(): stored = lax.all_to_all(pieces, MINOR, 0, 0)]
    all_to_all x0 -> x3, starting transfers between devices: none -> 24.8 us  [the longest x1 15.7 us: spread(): along = lax.all_to_all(copies, 'z', 0, 0)]
    slice x4 -> x2, local copies, waits for them, and re-layouts: 23.4 us -> 0.12 us  [the longest x1 0.07 us: body(): jnp.roll(weights.astype(jnp.bfloat16), span * own_rows, axis=-1)]
    all_to_all x0 -> x1, blocking collectives: none -> 14.8 us  [spread(): along = lax.all_to_all(copies, 'z', 0, 0)]
  transfers between devices with their start and end apart: 2 -> 4, of which waited for: 2 -> 4; matrix products, arithmetic and copies ran while one was open for 0% -> 3% of each run, Pallas kernels for 0% -> 0%
where the time goes in v1:
time: 125 us; the launch traced here: 124 us
  waiting for transfers between devices  55 us (44%)
  blocking collectives  30.4 us (24%)
  starting transfers between devices  28 us (22%)
  local copies, waits for them, and re-layouts  4.83 us (4%)
  matrix products  3.15 us (3%)
  other arithmetic  2.62 us (2%)
    all_to_all x1, waiting for transfers between devices, body(): stored = lax.all_to_all(pieces, MINOR, 0, 0)  26.8 us
    all_to_all x1, starting transfers between devices, spread(): along = lax.all_to_all(copies, 'z', 0, 0)  15.7 us
    all_gather x2, blocking collectives, spread(): full = lax.all_gather(along, ('x', 'c'))  15.5 us
    all_to_all x1, blocking collectives, spread(): along = lax.all_to_all(copies, 'z', 0, 0)  14.8 us
    all_to_all x1, waiting for transfers between devices, body(): fresh = lax.all_to_all(sent, MINOR, 0, 0)  13.4 us
    all_to_all x1, waiting for transfers between devices, spread(): along = lax.all_to_all(copies, 'z', 0, 0)  10 us
    ppermute x1, waiting for transfers between devices, body(): return lax.ppermute(updated, 'section', following)[None]  4.75 us
    all_to_all x1, starting transfers between devices, body(): fresh = lax.all_to_all(sent, MINOR, 0, 0)  4.55 us
  transfers between devices with their start and end apart: 4, of which 4 were waited for; matrix products, arithmetic and copies ran while one was open for 3% of the time, Pallas kernels for 0%

profile of v1, /device:TPU:1, one launch (start us, length us, event | category | flops | bytes accessed | tf_op | source)
XLA Modules:
  0.0 124.2 jit_solution(7751155175610397167)
XLA Ops:
  0.0 1.5 %broadcast_in_dim.31 = bf16[16,16,128]{2,1,0:T(8,128)(2,1)} broadcast(bf16[16,128]{1,0:T(8,128)(2,1)} %bitcast.72), dimensions={1,2} | broadcast | bytes 69632 | tf_op jit(solution)/shard_map/broadcast_in_dim | solution.py:34
  1.5 15.7 %all-to-all-start = ((bf16[16,16,128]{2,1,0:T(8,128)(2,1)}), bf16[16,16,128]{2,1,0:T(8,128)(2,1)S(1)}, u32[]{:S(2)}, u32[]{:S(2)}) async-start(bf16[16,16,128]{2,1,0:T(8,128)(2,1)} %broadcast_in_dim.31), calls=%async_computation | async-start | bytes 131072 | tf_op jit(solution)/shard_map/all_to_all | solution.py:35
  17.3 0.8 mul.174
  18.1 0.7 convert_bitcast_fusion
  18.7 10.0 %all-to-all-done = bf16[16,16,128]{2,1,0:T(8,128)(2,1)S(1)} async-done(((bf16[16,16,128]{2,1,0:T(8,128)(2,1)}), bf16[16,16,128]{2,1,0:T(8,128)(2,1)S(1)}, u32[]{:S(2)}, u32[]{:S(2)}) %all-to-all-start) | async-done | bytes 65568 | tf_op jit(solution)/shard_map/all_to_all | solution.py:35
  28.8 7.7 %all-gather = bf16[64,16,128]{2,1,0:T(8,128)(2,1)S(1)} all-gather(bf16[16,16,128]{2,1,0:T(8,128)(2,1)S(1)} %all-to-all-done), channel_id=2, replica_groups=mesh['section'=8,'x'=2,'z'=16,'c'=2] {'x','c'}, dimensions={0}, use_global_device_ids=true | all-gather | bytes 327680 | tf_op jit(solution)/shard_map/all_gather | solution.py:36
  36.5 0.2 fusion.13
  36.9 0.3 copy.22
  37.4 0.2 convolution_convert_fusion
  37.6 0.4 fusion.3
  38.4 0.7 broadcast_in_dim.34
  39.0 4.6 %all-to-all-start.1 = ((bf16[64,2,2,128]{3,2,1,0:T(2,128)(2,1)}), bf16[64,2,2,128]{3,2,1,0:T(2,128)(2,1)S(1)}, u32[]{:S(2)}, u32[]{:S(2)}) async-start(bf16[64,2,2,128]{3,2,1,0:T(2,128)(2,1)} %bitcast.11), calls=%async_computation.1 | async-start | bytes 131072 | tf_op jit(solution)/shard_map/all_to_all | solution.py:94
  43.7 1.1 copy.25
  44.8 13.4 %all-to-all-done.1 = bf16[64,2,2,128]{3,2,1,0:T(2,128)(2,1)S(1)} async-done(((bf16[64,2,2,128]{3,2,1,0:T(2,128)(2,1)}), bf16[64,2,2,128]{3,2,1,0:T(2,128)(2,1)S(1)}, u32[]{:S(2)}, u32[]{:S(2)}) %all-to-all-start.1) | async-done | bytes 65568 | tf_op jit(solution)/shard_map/all_to_all | solution.py:94
  58.2 4.5 %all-to-all-start.2 = ((bf16[64,24,128]{2,1,0:T(8,128)(2,1)}), bf16[64,24,128]{2,1,0:T(8,128)(2,1)S(1)}, u32[]{:S(2)}, u32[]{:S(2)}) async-start(bf16[64,24,128]{2,1,0:T(8,128)(2,1)} %bitcast.14), calls=%async_computation.2 | async-start | bytes 786432 | tf_op jit(solution)/shard_map/all_to_all | solution.py:63
  63.2 26.8 %all-to-all-done.2 = bf16[64,24,128]{2,1,0:T(8,128)(2,1)S(1)} async-done(((bf16[64,24,128]{2,1,0:T(8,128)(2,1)}), bf16[64,24,128]{2,1,0:T(8,128)(2,1)S(1)}, u32[]{:S(2)}, u32[]{:S(2)}) %all-to-all-start.2) | async-done | bytes 393248 | tf_op jit(solution)/shard_map/all_to_all | solution.py:63
  90.0 0.3 fusion.47
  90.6 0.2 fusion.9
  90.8 14.8 %all_to_all.20 = bf16[16,16,128]{2,1,0:T(8,128)(2,1)S(1)} all-to-all(bf16[16,16,128]{2,1,0:T(8,128)(2,1)S(1)} %broadcast_in_dim.37), channel_id=1, replica_groups=mesh['section'=8,'x'=2,'z'=16,'c'=2] {'z'}, dimensions={0} | all-to-all | bytes 131072 | tf_op jit(solution)/shard_map/all_to_all | solution.py:35
  105.7 7.8 %all-gather.1 = bf16[64,16,128]{2,1,0:T(8,128)(2,1)S(1)} all-gather(bf16[16,16,128]{2,1,0:T(8,128)(2,1)S(1)} %all_to_all.20), channel_id=3, replica_groups=mesh['section'=8,'x'=2,'z'=16,'c'=2] {'x','c'}, dimensions={0}, use_global_device_ids=true | all-gather | bytes 327680 | tf_op jit(solution)/shard_map/all_gather | solution.py:36
  113.7 2.0 %fusion.10 = bf16[16,128]{1,0:T(8,128)(2,1)S(1)} fusion(bf16[16,8192]{1,0:T(8,128)(2,1)S(1)} %reshape.233, bf16[1,8192,128]{2,1,0:T(8,128)(2,1)} %param.12, bf16[1,16,128]{2,1,0:T(8,128)(2,1)S(1)} %copy-done.3), kind=kOutput, calls=%fused_computation.11 | convolution fusion | flops 33560576 | bytes 2367488 | tf_op jit(solution)/shard_map/dot_general | solution.py:142
  115.7 3.2 %collective-permute-start = (bf16[16,128]{1,0:T(8,128)(2,1)S(1)}, bf16[16,128]{1,0:T(8,128)(2,1)S(1)}, u32[]{:S(2)}, u32[]{:S(2)}) collective-permute-start(bf16[16,128]{1,0:T(8,128)(2,1)S(1)} %fusion.10), channel_id=1, source_target_pairs={{0,64},{64,128},{128,192},{192,256},{256,320},{320,384},{384,448},... | collective-permute-start | bytes 12296 | tf_op jit(solution)/shard_map/ppermute | solution.py:146
  118.9 4.8 %collective-permute-done = bf16[16,128]{1,0:T(8,128)(2,1)S(1)} collective-permute-done((bf16[16,128]{1,0:T(8,128)(2,1)S(1)}, bf16[16,128]{1,0:T(8,128)(2,1)S(1)}, u32[]{:S(2)}, u32[]{:S(2)}) %collective-permute-start) | collective-permute-done | bytes 4128 | tf_op jit(solution)/shard_map/ppermute | solution.py:146
  123.6 0.6 copy.37
  (41 shorter events, 1.8 us)
Async XLA Ops:
  0.0 37.6 %copy-start = (bf16[1,8192,128]{2,1,0:T(8,128)(2,1)S(1)}, bf16[1,8192,128]{2,1,0:T(8,128)(2,1)}, u32[]{:S(2)}) copy-start(bf16[1,8192,128]{2,1,0:T(8,128)(2,1)} %param.10) | copy-start | bytes 6291460
  0.0 37.3 %copy-start.1 = (bf16[1,8192,32]{1,2,0:T(8,128)(2,1)S(1)}, bf16[1,8192,32]{1,2,0:T(8,128)(2,1)}, u32[]{:S(2)}) copy-start(bf16[1,8192,32]{1,2,0:T(8,128)(2,1)} %param.11) | copy-start | bytes 1572868
  1.5 27.3 %all-to-all-start = ((bf16[16,16,128]{2,1,0:T(8,128)(2,1)}), bf16[16,16,128]{2,1,0:T(8,128)(2,1)S(1)}, u32[]{:S(2)}, u32[]{:S(2)}) async-start(bf16[16,16,128]{2,1,0:T(8,128)(2,1)} %broadcast_in_dim.31), calls=%async_computation | async-start | bytes 131072 | tf_op jit(solution)/shard_map/all_to_all | solution.py:35
  37.1 6.5 %copy-start.2 = (bf16[1,16,6,2048]{3,1,2,0:T(8,128)(2,1)S(1)}, bf16[1,16,6,2048]{3,1,2,0:T(8,128)(2,1)}, u32[]{:S(2)}) copy-start(bf16[1,16,6,2048]{3,1,2,0:T(8,128)(2,1)} %param.13) | copy-start | bytes 1179652
  37.6 25.0 %copy-start.4 = (s32[1,16]{1,0:T(1,128)S(1)}, s32[1,16]{1,0:T(1,128)}, u32[]{:S(2)}) copy-start(s32[1,16]{1,0:T(1,128)} %param.14) | copy-start | bytes 196
  39.0 19.1 %all-to-all-start.1 = ((bf16[64,2,2,128]{3,2,1,0:T(2,128)(2,1)}), bf16[64,2,2,128]{3,2,1,0:T(2,128)(2,1)S(1)}, u32[]{:S(2)}, u32[]{:S(2)}) async-start(bf16[64,2,2,128]{3,2,1,0:T(2,128)(2,1)} %bitcast.11), calls=%async_computation.1 | async-start | bytes 131072 | tf_op jit(solution)/shard_map/all_to_all | solution.py:94
  43.7 70.0 %copy-start.3 = (bf16[1,16,128]{2,1,0:T(8,128)(2,1)S(1)}, bf16[1,16,128]{2,1,0:T(8,128)(2,1)}, u32[]{:S(2)}) copy-start(bf16[1,16,128]{2,1,0:T(8,128)(2,1)} %param.8) | copy-start | bytes 12292
  58.2 31.8 %all-to-all-start.2 = ((bf16[64,24,128]{2,1,0:T(8,128)(2,1)}), bf16[64,24,128]{2,1,0:T(8,128)(2,1)S(1)}, u32[]{:S(2)}, u32[]{:S(2)}) async-start(bf16[64,24,128]{2,1,0:T(8,128)(2,1)} %bitcast.14), calls=%async_computation.2 | async-start | bytes 786432 | tf_op jit(solution)/shard_map/all_to_all | solution.py:63
  115.7 8.0 %collective-permute-start = (bf16[16,128]{1,0:T(8,128)(2,1)S(1)}, bf16[16,128]{1,0:T(8,128)(2,1)S(1)}, u32[]{:S(2)}, u32[]{:S(2)}) collective-permute-start(bf16[16,128]{1,0:T(8,128)(2,1)S(1)} %fusion.10), channel_id=1, source_target_pairs={{0,64},{64,128},{128,192},{192,256},{256,320},{320,384},{384,448},... | collective-permute-start | bytes 12296 | tf_op jit(solution)/shard_map/ppermute | solution.py:146

commit v2 on v1

--- a/solution.py
+++ b/solution.py
@@ -58,9 +58,8 @@
 
     pieces = key_value_cache[0].reshape(members, own_rows, span, 2, groups, HEAD_WIDTH)
     pieces = pieces.transpose(4, 0, 3, 2, 1, 5).reshape(
-        devices, 2 * span * own_rows, HEAD_WIDTH
+        groups, members, 2 * span * own_rows, HEAD_WIDTH
     )
-    stored = lax.all_to_all(pieces, MINOR, 0, 0)
 
     gathered = spread(resid[0])
     widened = gathered.transpose(3, 0, 2, 1, 4).reshape(rows, -1).astype(jnp.float32)
@@ -81,17 +80,20 @@
     keyval = jnp.where(
         lane_share[None, :] == me % shares, jnp.tile(keyval, (1, shares)), jnp.bfloat16(0)
     )
-    own = jnp.stack(
+    own = jnp.concatenate(
         [
             query.reshape(members, own_rows, HEAD_WIDTH),
             keyval.reshape(members, own_rows, HEAD_WIDTH),
         ],
         axis=1,
     )
-    sent = jnp.broadcast_to(own[None], (groups,) + own.shape).reshape(
-        (devices,) + own.shape[1:]
-    )
-    fresh = lax.all_to_all(sent, MINOR, 0, 0)
+    sent = jnp.concatenate(
+        [pieces, jnp.broadcast_to(own[None], (groups,) + own.shape)], axis=2
+    ).reshape(devices, -1, 4, HEAD_WIDTH)
+    arrived = lax.all_to_all(sent, MINOR, 0, 0).reshape(devices, -1, HEAD_WIDTH)
+    per_device = arrived.shape[1]
+    cached = 2 * span * own_rows
+    fresh = arrived[:, cached:].reshape(devices, 2, own_rows, HEAD_WIDTH)
     queries = lax.dynamic_slice_in_dim(fresh[:, 0], group * members, members)
     fresh_key = lax.dynamic_slice_in_dim(fresh[:, 1], group * shares, shares)
     fresh_value = lax.dynamic_slice_in_dim(
@@ -104,14 +106,14 @@
     fresh_key = rotate(fresh_key, own_cosine, own_sine).astype(jnp.bfloat16)
 
     own_lengths = lax.dynamic_slice_in_dim(lengths[0], member * own_rows, own_rows)
-    entries = devices * 2 * span * own_rows
+    entries = devices * per_device
     entry = jnp.arange(entries, dtype=jnp.int32)
     entry_row = entry % own_rows
-    entry_slot = entry // (2 * span * own_rows) * span + entry // own_rows % span
-    is_key = entry // (span * own_rows) % 2 == 0
+    entry_slot = entry // per_device * span + entry % per_device // own_rows
+    is_key = entry % per_device < span * own_rows
     row_index = jnp.arange(own_rows, dtype=jnp.int32)[:, None]
     live = (is_key & (entry_row == row_index)) & (entry_slot < own_lengths[:, None])
-    flat = stored.reshape(entries, HEAD_WIDTH)
+    flat = arrived.reshape(entries, HEAD_WIDTH)
     factor = 1.0 / math.sqrt(HEAD_WIDTH)
     scores = (
         lax.dot_general(

time: 125 us -> 109 us (0.87)
  waiting for transfers between devices: 55 us -> 42.8 us
  starting transfers between devices: 28 us -> 23.5 us
    all_to_all x2 -> x1, waiting for transfers between devices: 40.2 us -> 29.2 us  [body(): arrived = lax.all_to_all(sent, MINOR, 0, 0).reshape(devices, -1, HEAD_WIDTH)]
    all_to_all x2 -> x1, starting transfers between devices: 9.01 us -> 4.55 us  [body(): arrived = lax.all_to_all(sent, MINOR, 0, 0).reshape(devices, -1, HEAD_WIDTH)]
  transfers between devices with their start and end apart: 4 -> 3, of which waited for: 4 -> 3; matrix products, arithmetic and copies ran while one was open for 3% -> 3% of each run, Pallas kernels for 0% -> 0%
where the time goes in v2:
time: 109 us
  waiting for transfers between devices  42.8 us (39%)
  blocking collectives  30.7 us (28%)
  starting transfers between devices  23.5 us (22%)
  local copies, waits for them, and re-layouts  5.58 us (5%)
  matrix products  3.19 us (3%)
  other arithmetic  2.68 us (2%)
    all_to_all x1, waiting for transfers between devices, body(): arrived = lax.all_to_all(sent, MINOR, 0, 0).reshape(devices, -1, HEAD_WIDTH)  29.2 us
    all_to_all x1, starting transfers between devices, spread(): along = lax.all_to_all(copies, 'z', 0, 0)  15.7 us
    all_gather x2, blocking collectives, spread(): full = lax.all_gather(along, ('x', 'c'))  15.6 us
    all_to_all x1, blocking collectives, spread(): along = lax.all_to_all(copies, 'z', 0, 0)  15.1 us
    all_to_all x1, waiting for transfers between devices, spread(): along = lax.all_to_all(copies, 'z', 0, 0)  8.81 us
    ppermute x1, waiting for transfers between devices, body(): return lax.ppermute(updated, 'section', following)[None]  4.75 us
    all_to_all x1, starting transfers between devices, body(): arrived = lax.all_to_all(sent, MINOR, 0, 0).reshape(devices, -1, HEAD_WIDTH)  4.55 us
    ppermute x1, starting transfers between devices, body(): return lax.ppermute(updated, 'section', following)[None]  3.21 us
  transfers between devices with their start and end apart: 3, of which 3 were waited for; matrix products, arithmetic and copies ran while one was open for 3% of the time, Pallas kernels for 0%

profile of v2, /device:TPU:1, one launch (start us, length us, event | category | flops | bytes accessed | tf_op | source)
XLA Modules:
  0.0 108.7 jit_solution(13959168159553216950)
XLA Ops:
  0.0 1.5 %broadcast_in_dim.31 = bf16[16,16,128]{2,1,0:T(8,128)(2,1)} broadcast(bf16[16,128]{1,0:T(8,128)(2,1)} %bitcast.78), dimensions={1,2} | broadcast | bytes 69632 | tf_op jit(solution)/shard_map/broadcast_in_dim | solution.py:34
  1.5 15.7 %all-to-all-start = ((bf16[16,16,128]{2,1,0:T(8,128)(2,1)}), bf16[16,16,128]{2,1,0:T(8,128)(2,1)S(1)}, u32[]{:S(2)}, u32[]{:S(2)}) async-start(bf16[16,16,128]{2,1,0:T(8,128)(2,1)} %broadcast_in_dim.31), calls=%async_computation | async-start | bytes 131072 | tf_op jit(solution)/shard_map/all_to_all | solution.py:35
  17.3 0.8 mul.174
  18.1 1.1 copy.32
  19.3 0.7 convert_bitcast_fusion
  20.0 8.8 %all-to-all-done = bf16[16,16,128]{2,1,0:T(8,128)(2,1)S(1)} async-done(((bf16[16,16,128]{2,1,0:T(8,128)(2,1)}), bf16[16,16,128]{2,1,0:T(8,128)(2,1)S(1)}, u32[]{:S(2)}, u32[]{:S(2)}) %all-to-all-start) | async-done | bytes 65568 | tf_op jit(solution)/shard_map/all_to_all | solution.py:35
  28.8 7.7 %all-gather = bf16[64,16,128]{2,1,0:T(8,128)(2,1)S(1)} all-gather(bf16[16,16,128]{2,1,0:T(8,128)(2,1)S(1)} %all-to-all-done), channel_id=2, replica_groups=mesh['section'=8,'x'=2,'z'=16,'c'=2] {'x','c'}, dimensions={0}, use_global_device_ids=true | all-gather | bytes 327680 | tf_op jit(solution)/shard_map/all_gather | solution.py:36
  36.5 0.2 fusion.13
  36.9 0.3 copy.25
  37.2 0.2 convert_element_type.73
  37.3 0.2 convolution_convert_fusion
  37.7 0.4 fusion.3
  38.6 1.1 %copy.28 = bf16[64,7,4,128]{3,2,1,0:T(4,128)(2,1)} copy(bf16[64,7,4,128]{3,0,2,1:T(8,128)(2,1)S(1)} %bitcast.69) | data formatting | bytes 917504 | tf_op jit(solution)/shard_map/reshape | solution.py:92
  39.7 4.6 %all-to-all-start.1 = ((bf16[64,7,4,128]{3,2,1,0:T(4,128)(2,1)}), bf16[64,7,4,128]{3,2,1,0:T(4,128)(2,1)S(1)}, u32[]{:S(2)}, u32[]{:S(2)}) async-start(bf16[64,7,4,128]{3,2,1,0:T(4,128)(2,1)} %copy.28), calls=%async_computation.1 | async-start | bytes 917504 | tf_op jit(solution)/shard_map/all_to_all | solution.py:93
  44.5 29.2 %all-to-all-done.1 = bf16[64,7,4,128]{3,2,1,0:T(4,128)(2,1)S(1)} async-done(((bf16[64,7,4,128]{3,2,1,0:T(4,128)(2,1)}), bf16[64,7,4,128]{3,2,1,0:T(4,128)(2,1)S(1)}, u32[]{:S(2)}, u32[]{:S(2)}) %all-to-all-start.1) | async-done | bytes 458784 | tf_op jit(solution)/shard_map/all_to_all | solution.py:93
  74.1 0.3 fusion.45
  74.5 0.2 fusion.18
  74.7 0.2 fusion.9
  75.0 15.1 %all_to_all.15 = bf16[16,16,128]{2,1,0:T(8,128)(2,1)S(1)} all-to-all(bf16[16,16,128]{2,1,0:T(8,128)(2,1)S(1)} %broadcast_in_dim.37), channel_id=1, replica_groups=mesh['section'=8,'x'=2,'z'=16,'c'=2] {'z'}, dimensions={0} | all-to-all | bytes 131072 | tf_op jit(solution)/shard_map/all_to_all | solution.py:35
  90.1 7.8 %all-gather.1 = bf16[64,16,128]{2,1,0:T(8,128)(2,1)S(1)} all-gather(bf16[16,16,128]{2,1,0:T(8,128)(2,1)S(1)} %all_to_all.15), channel_id=3, replica_groups=mesh['section'=8,'x'=2,'z'=16,'c'=2] {'x','c'}, dimensions={0}, use_global_device_ids=true | all-gather | bytes 327680 | tf_op jit(solution)/shard_map/all_gather | solution.py:36
  98.1 2.0 %fusion.10 = bf16[16,128]{1,0:T(8,128)(2,1)S(1)} fusion(bf16[16,8192]{1,0:T(8,128)(2,1)S(1)} %reshape.189, bf16[1,8192,128]{2,1,0:T(8,128)(2,1)} %param.12, bf16[1,16,128]{2,1,0:T(8,128)(2,1)S(1)} %copy-done.2), kind=kOutput, calls=%fused_computation.11 | convolution fusion | flops 33560576 | bytes 2367488 | tf_op jit(solution)/shard_map/dot_general | solution.py:144
  100.1 3.2 %collective-permute-start = (bf16[16,128]{1,0:T(8,128)(2,1)S(1)}, bf16[16,128]{1,0:T(8,128)(2,1)S(1)}, u32[]{:S(2)}, u32[]{:S(2)}) collective-permute-start(bf16[16,128]{1,0:T(8,128)(2,1)S(1)} %fusion.10), channel_id=1, source_target_pairs={{0,64},{64,128},{128,192},{192,256},{256,320},{320,384},{384,448},... | collective-permute-start | bytes 12296 | tf_op jit(solution)/shard_map/ppermute | solution.py:148
  103.3 4.8 %collective-permute-done = bf16[16,128]{1,0:T(8,128)(2,1)S(1)} collective-permute-done((bf16[16,128]{1,0:T(8,128)(2,1)S(1)}, bf16[16,128]{1,0:T(8,128)(2,1)S(1)}, u32[]{:S(2)}, u32[]{:S(2)}) %collective-permute-start) | collective-permute-done | bytes 4128 | tf_op jit(solution)/shard_map/ppermute | solution.py:148
  108.1 0.6 copy.34
  (41 shorter events, 1.7 us)
Async XLA Ops:
  0.0 37.7 %copy-start = (bf16[1,8192,128]{2,1,0:T(8,128)(2,1)S(1)}, bf16[1,8192,128]{2,1,0:T(8,128)(2,1)}, u32[]{:S(2)}) copy-start(bf16[1,8192,128]{2,1,0:T(8,128)(2,1)} %param.10) | copy-start | bytes 6291460
  0.0 37.3 %copy-start.1 = (bf16[1,8192,32]{1,2,0:T(8,128)(2,1)S(1)}, bf16[1,8192,32]{1,2,0:T(8,128)(2,1)}, u32[]{:S(2)}) copy-start(bf16[1,8192,32]{1,2,0:T(8,128)(2,1)} %param.11) | copy-start | bytes 1572868
  1.5 27.3 %all-to-all-start = ((bf16[16,16,128]{2,1,0:T(8,128)(2,1)}), bf16[16,16,128]{2,1,0:T(8,128)(2,1)S(1)}, u32[]{:S(2)}, u32[]{:S(2)}) async-start(bf16[16,16,128]{2,1,0:T(8,128)(2,1)} %broadcast_in_dim.31), calls=%async_computation | async-start | bytes 131072 | tf_op jit(solution)/shard_map/all_to_all | solution.py:35
  38.1 6.2 %copy-start.3 = (s32[1,16]{1,0:T(1,128)S(1)}, s32[1,16]{1,0:T(1,128)}, u32[]{:S(2)}) copy-start(s32[1,16]{1,0:T(1,128)} %param.14) | copy-start | bytes 196
  39.7 34.0 %all-to-all-start.1 = ((bf16[64,7,4,128]{3,2,1,0:T(4,128)(2,1)}), bf16[64,7,4,128]{3,2,1,0:T(4,128)(2,1)S(1)}, u32[]{:S(2)}, u32[]{:S(2)}) async-start(bf16[64,7,4,128]{3,2,1,0:T(4,128)(2,1)} %copy.28), calls=%async_computation.1 | async-start | bytes 917504 | tf_op jit(solution)/shard_map/all_to_all | solution.py:93
  44.3 53.9 %copy-start.2 = (bf16[1,16,128]{2,1,0:T(8,128)(2,1)S(1)}, bf16[1,16,128]{2,1,0:T(8,128)(2,1)}, u32[]{:S(2)}) copy-start(bf16[1,16,128]{2,1,0:T(8,128)(2,1)} %param.8) | copy-start | bytes 12292
  100.1 8.0 %collective-permute-start = (bf16[16,128]{1,0:T(8,128)(2,1)S(1)}, bf16[16,128]{1,0:T(8,128)(2,1)S(1)}, u32[]{:S(2)}, u32[]{:S(2)}) collective-permute-start(bf16[16,128]{1,0:T(8,128)(2,1)S(1)} %fusion.10), channel_id=1, source_target_pairs={{0,64},{64,128},{128,192},{192,256},{256,320},{320,384},{384,448},... | collective-permute-start | bytes 12296 | tf_op jit(solution)/shard_map/ppermute | solution.py:148

commit v3 on v2

--- a/solution.py
+++ b/solution.py
@@ -1,8 +1,11 @@
+import functools
 import math
 
 import jax
 import jax.numpy as jnp
 from jax import lax
+from jax.experimental import pallas as pl
+from jax.experimental.pallas import tpu as pltpu
 from jax.sharding import Mesh
 from jax.sharding import PartitionSpec as P
 
@@ -35,6 +38,45 @@
     along = lax.all_to_all(copies, "z", 0, 0)
     full = lax.all_gather(along, ("x", "c"))
     return full.reshape((lax.axis_size("x"), lax.axis_size("c"), line) + part.shape)
+
+
+def place_rows(cores, line, gathered_ref, gain_ref, query_ref, keyval_ref, cosine_ref, sine_ref,
+               share_ref, out_ref, normed_ref):
+    rows, width = gathered_ref.shape[1:]
+    squares = jnp.zeros((rows, width), jnp.float32)
+    for at in range(gathered_ref.shape[0]):
+        wide = gathered_ref[at].astype(jnp.float32)
+        squares = squares + wide * wide
+    meansq = jnp.sum(squares, axis=-1, keepdims=True) / (gathered_ref.shape[0] * width)
+    scale = lax.rsqrt(meansq + 1e-05)
+    for at in range(gathered_ref.shape[0]):
+        side, core, chip = at // (cores * line), at // line % cores, at % line
+        first = ((side * line + chip) * cores + core) * width
+        gain = gain_ref[:, first : first + width].astype(jnp.float32)
+        wide = gathered_ref[at].astype(jnp.float32)
+        normed_ref[:, first : first + width] = (wide * scale * gain).astype(jnp.bfloat16)
+    normed = normed_ref[...]
+    query = jnp.dot(normed, query_ref[...], preferred_element_type=jnp.float32)
+    keyval = lax.dot_general(
+        normed, keyval_ref[...], (((1,), (1,)), ((), ())), preferred_element_type=jnp.float32
+    ).astype(jnp.bfloat16)
+    query = query * cosine_ref[...] + pltpu.roll(query, width // 2, 1) * sine_ref[...]
+    part = keyval.shape[1]
+    lane = lax.broadcasted_iota(jnp.int32, (part, width), 1)
+    column = lax.broadcasted_iota(jnp.int32, (part, width), 0)
+    place = jnp.where(lane == column + share_ref[0] * part, 1.0, 0.0).astype(jnp.bfloat16)
+    placed = jnp.dot(keyval, place, preferred_element_type=jnp.float32).astype(jnp.bfloat16)
+    both = jnp.concatenate([query.astype(jnp.bfloat16), placed], axis=0)
+    to = lax.broadcasted_iota(jnp.int32, (2 * rows, 2 * rows), 0)
+    source = lax.broadcasted_iota(jnp.int32, (2 * rows, 2 * rows), 1)
+    wanted = (to // 4) * 2 + to % 2 + jnp.where(to % 4 >= 2, rows, 0)
+    order = jnp.where(source == wanted, 1.0, 0.0).astype(jnp.bfloat16)
+    out_ref[...] = jnp.dot(order, both, preferred_element_type=jnp.float32).astype(jnp.bfloat16)
+
+
+def add_product(attn_ref, weight_ref, resid_ref, out_ref):
+    product = jnp.dot(attn_ref[...], weight_ref[...], preferred_element_type=jnp.float32)
+    out_ref[...] = (resid_ref[...].astype(jnp.float32) + product).astype(out_ref.dtype)
 
 
 def body(
@@ -58,38 +100,37 @@
 
     pieces = key_value_cache[0].reshape(members, own_rows, span, 2, groups, HEAD_WIDTH)
     pieces = pieces.transpose(4, 0, 3, 2, 1, 5).reshape(
-        groups, members, 2 * span * own_rows, HEAD_WIDTH
-    )
+        devices, span, 2 * own_rows, HEAD_WIDTH
+    )
+    pieces = lax.optimization_barrier(jnp.pad(pieces, ((0, 0), (0, 1), (0, 0), (0, 0))))
 
     gathered = spread(resid[0])
-    widened = gathered.transpose(3, 0, 2, 1, 4).reshape(rows, -1).astype(jnp.float32)
-    meansq = jnp.mean(widened * widened, axis=-1, keepdims=True)
-    normed = (widened * lax.rsqrt(meansq + 1e-05) * norm_gain[0].astype(jnp.float32)).astype(
-        jnp.bfloat16
-    )
+    side, cores, line = gathered.shape[:3]
     cosine, sine = rotary_tables(positions[0])
-    query = rotate(
-        jnp.dot(normed, query_weight[0], preferred_element_type=jnp.float32), cosine, sine
-    ).astype(jnp.bfloat16)
-    keyval = jnp.dot(normed, key_value_weight[0], preferred_element_type=jnp.float32).astype(
-        jnp.bfloat16
-    )
-    width = keyval.shape[1]
+    width = key_value_weight.shape[2]
     shares = HEAD_WIDTH // width
-    lane_share = jnp.arange(HEAD_WIDTH, dtype=jnp.int32) // width
-    keyval = jnp.where(
-        lane_share[None, :] == me % shares, jnp.tile(keyval, (1, shares)), jnp.bfloat16(0)
-    )
-    own = jnp.concatenate(
-        [
-            query.reshape(members, own_rows, HEAD_WIDTH),
-            keyval.reshape(members, own_rows, HEAD_WIDTH),
-        ],
-        axis=1,
-    )
-    sent = jnp.concatenate(
-        [pieces, jnp.broadcast_to(own[None], (groups,) + own.shape)], axis=2
-    ).reshape(devices, -1, 4, HEAD_WIDTH)
+    whole, small = pl.BlockSpec(memory_space=pltpu.VMEM), pl.BlockSpec(memory_space=pltpu.SMEM)
+    own = pl.pallas_call(
+        functools.partial(place_rows, cores, line),
+        out_shape=jax.ShapeDtypeStruct((2 * rows, HEAD_WIDTH), jnp.bfloat16),
+        in_specs=[whole] * 6 + [small],
+        out_specs=whole,
+        scratch_shapes=[pltpu.VMEM((rows, query_weight.shape[1]), jnp.bfloat16)],
+        compiler_params=pltpu.CompilerParams(vmem_limit_bytes=24 * 2**20),
+    )(
+        gathered.reshape((devices,) + resid.shape[1:]),
+        norm_gain,
+        query_weight[0],
+        key_value_weight[0].T,
+        jnp.concatenate([cosine, cosine], axis=1),
+        jnp.concatenate([-sine, sine], axis=1),
+        (me % shares).reshape(1),
+    )
+    own = own.reshape(members, 2 * own_rows, HEAD_WIDTH)
+    own = jnp.broadcast_to(own[None], (groups,) + own.shape).reshape(
+        devices, 1, 2 * own_rows, HEAD_WIDTH
+    )
+    sent = lax.dynamic_update_slice_in_dim(pieces, own, pieces.shape[1] - 1, axis=1)
     arrived = lax.all_to_all(sent, MINOR, 0, 0).reshape(devices, -1, HEAD_WIDTH)
     per_device = arrived.shape[1]
     cached = 2 * span * own_rows
@@ -141,8 +182,13 @@
     inner = members // c
     full = full.reshape(x, c, line // inner, inner, members, own_rows, HEAD_WIDTH)
     full = full.transpose(3, 1, 5, 0, 2, 4, 6).reshape(rows, -1)
-    projected = jnp.dot(full, out_weight[0], preferred_element_type=jnp.float32)
-    updated = (resid[0].astype(jnp.float32) + projected).astype(jnp.bfloat16)
+    updated = pl.pallas_call(
+        add_product,
+        out_shape=jax.ShapeDtypeStruct(resid.shape[1:], resid.dtype),
+        in_specs=[whole] * 3,
+        out_specs=whole,
+        compiler_params=pltpu.CompilerParams(vmem_limit_bytes=24 * 2**20),
+    )(full, out_weight[0], resid[0])
     sections = lax.axis_size("section")
     following = [(i, (i + 1) % sections) for i in range(sections)]
     return lax.ppermute(updated, "section", following)[None]

time: 109 us -> 106 us (0.972)
  matrix products: 3.19 us -> 0.58 us
  Pallas kernels: 0 us -> 1.27 us
  other arithmetic: 2.68 us -> 1.46 us
    dot_general x3 -> x0, matrix products: 2.61 us -> none  [the longest x1 1.98 us: body(): projected = jnp.dot(full, out_weight[0], preferred_element_type=jnp.float32)]
    pallas_call x0 -> x2, Pallas kernels: none -> 1.27 us  [the longest x1 0.89 us: body(): pl.pallas_call(functools.partial(place_rows, cores, line), out_shape=jax....]
    reshape x1 -> x0, local copies, waits for them, and re-layouts: 1.13 us -> none  [body(): sent = jnp.concatenate([pieces, jnp.broadcast_to(own[None], (groups,) + o...]
where the time goes in v3:
time: 106 us
  waiting for transfers between devices  42.3 us (40%)
  blocking collectives  30.6 us (29%)
  starting transfers between devices  23.5 us (22%)
  local copies, waits for them, and re-layouts  5.51 us (5%)
  other arithmetic  1.46 us (1%)
  Pallas kernels  1.27 us (1%)
    all_to_all x1, waiting for transfers between devices, body(): arrived = lax.all_to_all(sent, MINOR, 0, 0).reshape(devices, -1, HEAD_WIDTH)  29.2 us
    all_to_all x1, starting transfers between devices, spread(): along = lax.all_to_all(copies, 'z', 0, 0)  15.7 us
    all_gather x2, blocking collectives, spread(): full = lax.all_gather(along, ('x', 'c'))  15.5 us
    all_to_all x1, blocking collectives, spread(): along = lax.all_to_all(copies, 'z', 0, 0)  15.1 us
    all_to_all x1, waiting for transfers between devices, spread(): along = lax.all_to_all(copies, 'z', 0, 0)  8.38 us
    ppermute x1, waiting for transfers between devices, body(): return lax.ppermute(updated, 'section', following)[None]  4.75 us
    all_to_all x1, starting transfers between devices, body(): arrived = lax.all_to_all(sent, MINOR, 0, 0).reshape(devices, -1, HEAD_WIDTH)  4.55 us
    ppermute x1, starting transfers between devices, body(): return lax.ppermute(updated, 'section', following)[None]  3.21 us
  transfers between devices with their start and end apart: 3, of which 3 were waited for; matrix products, arithmetic and copies ran while one was open for 3% of the time, Pallas kernels for 0%

profile of v3, /device:TPU:1, one launch (start us, length us, event | category | flops | bytes accessed | tf_op | source)
XLA Modules:
  0.0 105.5 jit_solution(7831300342320295245)
XLA Ops:
  0.0 1.5 %broadcast_in_dim.24 = bf16[16,16,128]{2,1,0:T(8,128)(2,1)} broadcast(bf16[16,128]{1,0:T(8,128)(2,1)} %bitcast.48), dimensions={1,2} | broadcast | bytes 69632 | tf_op jit(solution)/shard_map/broadcast_in_dim | solution.py:37
  1.5 15.7 %all-to-all-start = ((bf16[16,16,128]{2,1,0:T(8,128)(2,1)}), bf16[16,16,128]{2,1,0:T(8,128)(2,1)S(1)}, u32[]{:S(2)}, u32[]{:S(2)}) async-start(bf16[16,16,128]{2,1,0:T(8,128)(2,1)} %broadcast_in_dim.24), calls=%async_computation | async-start | bytes 131072 | tf_op jit(solution)/shard_map/all_to_all | solution.py:38
  17.3 0.7 convert_bitcast_fusion
  17.9 1.1 %copy.20 = bf16[12,8,16,128]{3,2,1,0:T(8,128)(2,1)S(1)} copy(bf16[12,8,16,128]{3,1,2,0:T(8,128)(2,1)} %bitcast.56) | data formatting | bytes 786432
  19.0 0.3 copy.16
  19.3 0.9 pad.4
  20.2 0.1 fusion.24
  20.4 8.4 %all-to-all-done = bf16[16,16,128]{2,1,0:T(8,128)(2,1)S(1)} async-done(((bf16[16,16,128]{2,1,0:T(8,128)(2,1)}), bf16[16,16,128]{2,1,0:T(8,128)(2,1)S(1)}, u32[]{:S(2)}, u32[]{:S(2)}) %all-to-all-start) | async-done | bytes 65568 | tf_op jit(solution)/shard_map/all_to_all | solution.py:38
  28.8 7.7 %all-gather.gathered_ref = bf16[64,16,128]{2,1,0:T(8,128)(2,1)S(1)} all-gather(bf16[16,16,128]{2,1,0:T(8,128)(2,1)S(1)} %all-to-all-done), channel_id=2, replica_groups=mesh['section'=8,'x'=2,'z'=16,'c'=2] {'x','c'}, dimensions={0}, use_global_device_ids=true | all-gather | bytes 327680 | tf_op jit(solution)/shard_map/all_gather | solution.py:39
  36.5 0.9 shard_map.82
  37.5 0.7 constant_dynamic-update-slice_fusion
  38.1 4.5 %all-to-all-start.1 = ((bf16[64,7,4,128]{3,2,1,0:T(4,128)(2,1)}), bf16[64,7,4,128]{3,2,1,0:T(4,128)(2,1)S(1)}, u32[]{:S(2)}, u32[]{:S(2)}) async-start(bf16[64,7,4,128]{3,2,1,0:T(4,128)(2,1)} %constant_dynamic-update-slice_fusion), calls=%async_computation.1 | async-start | bytes 917504 | tf_op jit(solution)/shard_map/all_to_all | solution.py:134
  43.0 29.2 %all-to-all-done.1 = bf16[64,7,4,128]{3,2,1,0:T(4,128)(2,1)S(1)} async-done(((bf16[64,7,4,128]{3,2,1,0:T(4,128)(2,1)}), bf16[64,7,4,128]{3,2,1,0:T(4,128)(2,1)S(1)}, u32[]{:S(2)}, u32[]{:S(2)}) %all-to-all-start.1) | async-done | bytes 458784 | tf_op jit(solution)/shard_map/all_to_all | solution.py:134
  72.2 0.1 copy.17
  72.6 0.3 fusion.30
  72.9 0.2 fusion.3
  73.2 0.2 fusion.2
  73.5 15.1 %all_to_all.15 = bf16[16,16,128]{2,1,0:T(8,128)(2,1)S(1)} all-to-all(bf16[16,16,128]{2,1,0:T(8,128)(2,1)S(1)} %broadcast_in_dim.51), channel_id=1, replica_groups=mesh['section'=8,'x'=2,'z'=16,'c'=2] {'z'}, dimensions={0} | all-to-all | bytes 131072 | tf_op jit(solution)/shard_map/all_to_all | solution.py:38
  88.6 7.8 %all-gather.1 = bf16[64,16,128]{2,1,0:T(8,128)(2,1)S(1)} all-gather(bf16[16,16,128]{2,1,0:T(8,128)(2,1)S(1)} %all_to_all.15), channel_id=3, replica_groups=mesh['section'=8,'x'=2,'z'=16,'c'=2] {'x','c'}, dimensions={0}, use_global_device_ids=true | all-gather | bytes 327680 | tf_op jit(solution)/shard_map/all_gather | solution.py:39
  96.5 0.1 reshape.127.attn_ref
  96.6 0.4 shard_map.83
  97.0 3.2 %collective-permute-start = (bf16[16,128]{1,0:T(8,128)(2,1)S(1)}, bf16[16,128]{1,0:T(8,128)(2,1)S(1)}, u32[]{:S(2)}, u32[]{:S(2)}) collective-permute-start(bf16[16,128]{1,0:T(8,128)(2,1)S(1)} %shard_map.83), channel_id=1, source_target_pairs={{0,64},{64,128},{128,192},{192,256},{256,320},{320,384},{384,448},... | collective-permute-start | bytes 12296 | tf_op jit(solution)/shard_map/ppermute | solution.py:194
  100.2 4.8 %collective-permute-done = bf16[16,128]{1,0:T(8,128)(2,1)S(1)} collective-permute-done((bf16[16,128]{1,0:T(8,128)(2,1)S(1)}, bf16[16,128]{1,0:T(8,128)(2,1)S(1)}, u32[]{:S(2)}, u32[]{:S(2)}) %collective-permute-start) | collective-permute-done | bytes 4128 | tf_op jit(solution)/shard_map/ppermute | solution.py:194
  105.0 0.6 copy.23
  (31 shorter events, 0.8 us)
Async XLA Ops:
  0.0 42.8 %copy-start = (s32[1,16]{1,0:T(1,128)S(1)}, s32[1,16]{1,0:T(1,128)}, u32[]{:S(2)}) copy-start(s32[1,16]{1,0:T(1,128)} %param.14) | copy-start | bytes 196
  0.0 36.5 %copy-start.1 = (bf16[1,8192,128]{2,1,0:T(8,128)(2,1)S(1)}, bf16[1,8192,128]{2,1,0:T(8,128)(2,1)}, u32[]{:S(2)}) copy-start(bf16[1,8192,128]{2,1,0:T(8,128)(2,1)} %param.10) | copy-start | bytes 6291460
  0.0 36.5 %copy-start.3 = (bf16[1,8192,32]{1,2,0:T(8,128)(2,1)S(1)}, bf16[1,8192,32]{1,2,0:T(8,128)(2,1)}, u32[]{:S(2)}) copy-start(bf16[1,8192,32]{1,2,0:T(8,128)(2,1)} %param.11) | copy-start | bytes 1572868
  0.0 36.5 %copy-start.4 = (bf16[1,8192]{1,0:T(2,128)(2,1)S(1)}, bf16[1,8192]{1,0:T(2,128)(2,1)}, u32[]{:S(2)}) copy-start(bf16[1,8192]{1,0:T(2,128)(2,1)} %gain_ref.1) | copy-start | bytes 49156
  1.5 27.3 %all-to-all-start = ((bf16[16,16,128]{2,1,0:T(8,128)(2,1)}), bf16[16,16,128]{2,1,0:T(8,128)(2,1)S(1)}, u32[]{:S(2)}, u32[]{:S(2)}) async-start(bf16[16,16,128]{2,1,0:T(8,128)(2,1)} %broadcast_in_dim.24), calls=%async_computation | async-start | bytes 131072 | tf_op jit(solution)/shard_map/all_to_all | solution.py:38
  38.1 34.0 %all-to-all-start.1 = ((bf16[64,7,4,128]{3,2,1,0:T(4,128)(2,1)}), bf16[64,7,4,128]{3,2,1,0:T(4,128)(2,1)S(1)}, u32[]{:S(2)}, u32[]{:S(2)}) async-start(bf16[64,7,4,128]{3,2,1,0:T(4,128)(2,1)} %constant_dynamic-update-slice_fusion), calls=%async_computation.1 | async-start | bytes 917504 | tf_op jit(solution)/shard_map/all_to_all | solution.py:134
  42.7 53.9 %copy-start.2 = (bf16[1,8192,128]{2,1,0:T(8,128)(2,1)S(1)}, bf16[1,8192,128]{2,1,0:T(8,128)(2,1)}, u32[]{:S(2)}) copy-start(bf16[1,8192,128]{2,1,0:T(8,128)(2,1)} %param.12) | copy-start | bytes 6291460
  42.7 53.9 %copy-start.5 = (bf16[1,16,128]{2,1,0:T(8,128)(2,1)S(1)}, bf16[1,16,128]{2,1,0:T(8,128)(2,1)}, u32[]{:S(2)}) copy-start(bf16[1,16,128]{2,1,0:T(8,128)(2,1)} %param.8) | copy-start | bytes 12292
  97.0 8.0 %collective-permute-start = (bf16[16,128]{1,0:T(8,128)(2,1)S(1)}, bf16[16,128]{1,0:T(8,128)(2,1)S(1)}, u32[]{:S(2)}, u32[]{:S(2)}) collective-permute-start(bf16[16,128]{1,0:T(8,128)(2,1)S(1)} %shard_map.83), channel_id=1, source_target_pairs={{0,64},{64,128},{128,192},{192,256},{256,320},{320,384},{384,448},... | collective-permute-start | bytes 12296 | tf_op jit(solution)/shard_map/ppermute | solution.py:194

commit v4 on v3

--- a/solution.py
+++ b/solution.py
@@ -21,15 +21,6 @@
     )
     angles = token_positions.astype(jnp.float32)[:, None] * freqs
     return jnp.cos(angles), jnp.sin(angles)
-
-
-def rotate(vectors, cosine, sine):
-    half_size = vectors.shape[-1] // 2
-    first = vectors[..., :half_size]
-    second = vectors[..., half_size:]
-    return jnp.concatenate(
-        [first * cosine - second * sine, second * cosine + first * sine], axis=-1
-    )
 
 
 def spread(part):
@@ -74,6 +65,31 @@
     out_ref[...] = jnp.dot(order, both, preferred_element_type=jnp.float32).astype(jnp.bfloat16)
 
 
+def attend(span, factor, entries_ref, select_ref, bias_ref, cosine_ref, sine_ref, out_ref):
+    entries = entries_ref[...]
+    rows, width = out_ref.shape
+    picked = jnp.dot(select_ref[...], entries, preferred_element_type=jnp.float32)
+    query, fresh_key, fresh_value = picked[:rows], picked[rows : 2 * rows], picked[2 * rows :]
+    scores = lax.dot_general(
+        query.astype(jnp.bfloat16),
+        entries,
+        (((1,), (1,)), ((), ())),
+        preferred_element_type=jnp.float32,
+    )
+    scores = scores * factor + bias_ref[...]
+    fresh_key = fresh_key * cosine_ref[...] + pltpu.roll(fresh_key, width // 2, 1) * sine_ref[...]
+    fresh_key = fresh_key.astype(jnp.bfloat16).astype(jnp.float32)
+    new_score = jnp.sum(query * fresh_key, axis=-1, keepdims=True) * factor
+    peak = jnp.maximum(jnp.max(scores, axis=-1, keepdims=True), new_score)
+    weights = jnp.exp(scores - peak)
+    new_weight = jnp.exp(new_score - peak)
+    totals = jnp.sum(weights, axis=-1, keepdims=True) + new_weight
+    weights = pltpu.roll(weights, span, 1).astype(jnp.bfloat16)
+    mixture = jnp.dot(weights, entries, preferred_element_type=jnp.float32)
+    mixture = mixture + new_weight * fresh_value
+    out_ref[...] = (mixture / totals).astype(jnp.bfloat16)
+
+
 def add_product(attn_ref, weight_ref, resid_ref, out_ref):
     product = jnp.dot(attn_ref[...], weight_ref[...], preferred_element_type=jnp.float32)
     out_ref[...] = (resid_ref[...].astype(jnp.float32) + product).astype(out_ref.dtype)
@@ -134,50 +150,45 @@
     arrived = lax.all_to_all(sent, MINOR, 0, 0).reshape(devices, -1, HEAD_WIDTH)
     per_device = arrived.shape[1]
     cached = 2 * span * own_rows
-    fresh = arrived[:, cached:].reshape(devices, 2, own_rows, HEAD_WIDTH)
-    queries = lax.dynamic_slice_in_dim(fresh[:, 0], group * members, members)
-    fresh_key = lax.dynamic_slice_in_dim(fresh[:, 1], group * shares, shares)
-    fresh_value = lax.dynamic_slice_in_dim(
-        fresh[:, 1], devices // 2 + group * shares, shares
-    )
-    fresh_key = fresh_key.astype(jnp.float32).sum(0)
-    fresh_value = fresh_value.astype(jnp.float32).sum(0)
+    entries = devices * per_device
+
+    own_lengths = lax.dynamic_slice_in_dim(lengths[0], member * own_rows, own_rows)
     own_cosine = lax.dynamic_slice_in_dim(cosine, member * own_rows, own_rows)
     own_sine = lax.dynamic_slice_in_dim(sine, member * own_rows, own_rows)
-    fresh_key = rotate(fresh_key, own_cosine, own_sine).astype(jnp.bfloat16)
-
-    own_lengths = lax.dynamic_slice_in_dim(lengths[0], member * own_rows, own_rows)
-    entries = devices * per_device
     entry = jnp.arange(entries, dtype=jnp.int32)
-    entry_row = entry % own_rows
-    entry_slot = entry // per_device * span + entry % per_device // own_rows
-    is_key = entry % per_device < span * own_rows
-    row_index = jnp.arange(own_rows, dtype=jnp.int32)[:, None]
-    live = (is_key & (entry_row == row_index)) & (entry_slot < own_lengths[:, None])
-    flat = arrived.reshape(entries, HEAD_WIDTH)
-    factor = 1.0 / math.sqrt(HEAD_WIDTH)
-    scores = (
-        lax.dot_general(
-            queries, flat, (((2,), (1,)), ((), ())), preferred_element_type=jnp.float32
-        )
-        * factor
-    )
-    new_score = (queries.astype(jnp.float32) * fresh_key.astype(jnp.float32)).sum(-1) * factor
-    scores = jnp.where(live, scores, -1e30)
-    peak = jnp.maximum(scores.max(-1), new_score)
-    weights = jnp.exp(scores - peak[..., None])
-    new_weight = jnp.exp(new_score - peak)
-    totals = weights.sum(-1) + new_weight
-    mixture = lax.dot_general(
-        jnp.roll(weights.astype(jnp.bfloat16), span * own_rows, axis=-1),
-        flat,
-        (((2,), (0,)), ((), ())),
-        preferred_element_type=jnp.float32,
-    )
-    mixture = mixture + new_weight[..., None] * fresh_value
-    attn = (mixture / totals[..., None]).astype(jnp.bfloat16)
-
-    full = spread(attn.reshape(members * own_rows, HEAD_WIDTH))
+    entry_from, entry_at = entry // per_device, entry % per_device
+    entry_row = entry_at % own_rows
+    entry_slot = entry_from * span + entry_at // own_rows
+    rank = jnp.arange(members * own_rows, dtype=jnp.int32)[:, None]
+    rank_row = rank % own_rows
+    is_query = (entry_at >= cached) & (entry_at < cached + own_rows)
+    is_fresh = entry_at >= cached + own_rows
+    select = [
+        is_query & (entry_from == group * members + rank // own_rows),
+        is_fresh & (entry_from // shares == group),
+        is_fresh & (entry_from // shares == groups + group),
+    ]
+    select = jnp.concatenate([part & (entry_row == rank_row) for part in select]).astype(
+        jnp.bfloat16
+    )
+    live = (entry_at < span * own_rows) & (entry_row == rank_row)
+    live = live & (entry_slot < jnp.tile(own_lengths, members)[:, None])
+    bias = jnp.where(live, 0.0, -1e30)
+    attn = pl.pallas_call(
+        functools.partial(attend, span * own_rows, 1.0 / math.sqrt(HEAD_WIDTH)),
+        out_shape=jax.ShapeDtypeStruct((members * own_rows, HEAD_WIDTH), jnp.bfloat16),
+        in_specs=[whole] * 5,
+        out_specs=whole,
+        compiler_params=pltpu.CompilerParams(vmem_limit_bytes=24 * 2**20),
+    )(
+        arrived.reshape(entries, HEAD_WIDTH),
+        select,
+        bias,
+        jnp.tile(jnp.concatenate([own_cosine, own_cosine], axis=1), (members, 1)),
+        jnp.tile(jnp.concatenate([-own_sine, own_sine], axis=1), (members, 1)),
+    )
+
+    full = spread(attn)
     x, c, line = full.shape[:3]
     inner = members // c
     full = full.reshape(x, c, line // inner, inner, members, own_rows, HEAD_WIDTH)

time: 106 us -> 105 us (level)
  transfers between devices with their start and end apart: 3 -> 3, of which waited for: 3 -> 3; matrix products, arithmetic and copies ran while one was open for 3% -> 4% of each run, Pallas kernels for 0% -> 0%
where the time goes in v4:
time: 105 us
  waiting for transfers between devices  41.8 us (40%)
  blocking collectives  30.6 us (29%)
  starting transfers between devices  23.5 us (22%)
  local copies, waits for them, and re-layouts  5.42 us (5%)
  Pallas kernels  2.02 us (2%)
  other arithmetic  1.38 us (1%)
    all_to_all x1, waiting for transfers between devices, body(): arrived = lax.all_to_all(sent, MINOR, 0, 0).reshape(devices, -1, HEAD_WIDTH)  28.8 us
    all_to_all x1, starting transfers between devices, spread(): along = lax.all_to_all(copies, 'z', 0, 0)  15.7 us
    all_gather x2, blocking collectives, spread(): full = lax.all_gather(along, ('x', 'c'))  15.6 us
    all_to_all x1, blocking collectives, spread(): along = lax.all_to_all(copies, 'z', 0, 0)  15.1 us
    all_to_all x1, waiting for transfers between devices, spread(): along = lax.all_to_all(copies, 'z', 0, 0)  8.21 us
    ppermute x1, waiting for transfers between devices, body(): return lax.ppermute(updated, 'section', following)[None]  4.75 us
    all_to_all x1, starting transfers between devices, body(): arrived = lax.all_to_all(sent, MINOR, 0, 0).reshape(devices, -1, HEAD_WIDTH)  4.55 us
    ppermute x1, starting transfers between devices, body(): return lax.ppermute(updated, 'section', following)[None]  3.21 us
  transfers between devices with their start and end apart: 3, of which 3 were waited for; matrix products, arithmetic and copies ran while one was open for 4% of the time, Pallas kernels for 0%

profile of v4, /device:TPU:1, one launch (start us, length us, event | category | flops | bytes accessed | tf_op | source)
XLA Modules:
  0.0 105.0 jit_solution(1699313986283347607)
XLA Ops:
  0.0 1.5 %broadcast_in_dim.19 = bf16[16,16,128]{2,1,0:T(8,128)(2,1)} broadcast(bf16[16,128]{1,0:T(8,128)(2,1)} %bitcast.39), dimensions={1,2} | broadcast | bytes 69632 | tf_op jit(solution)/shard_map/broadcast_in_dim | solution.py:28
  1.5 15.7 %all-to-all-start = ((bf16[16,16,128]{2,1,0:T(8,128)(2,1)}), bf16[16,16,128]{2,1,0:T(8,128)(2,1)S(1)}, u32[]{:S(2)}, u32[]{:S(2)}) async-start(bf16[16,16,128]{2,1,0:T(8,128)(2,1)} %broadcast_in_dim.19), calls=%async_computation | async-start | bytes 131072 | tf_op jit(solution)/shard_map/all_to_all | solution.py:29
  17.3 0.7 convert_bitcast_fusion
  18.0 0.1 fusion.18
  18.1 1.1 %copy.14 = bf16[12,8,16,128]{3,2,1,0:T(8,128)(2,1)S(1)} copy(bf16[12,8,16,128]{3,1,2,0:T(8,128)(2,1)} %bitcast.44) | data formatting | bytes 786432
  19.2 0.3 copy.12
  19.5 0.9 pad.4
  20.6 8.2 %all-to-all-done = bf16[16,16,128]{2,1,0:T(8,128)(2,1)S(1)} async-done(((bf16[16,16,128]{2,1,0:T(8,128)(2,1)}), bf16[16,16,128]{2,1,0:T(8,128)(2,1)S(1)}, u32[]{:S(2)}, u32[]{:S(2)}) %all-to-all-start) | async-done | bytes 65568 | tf_op jit(solution)/shard_map/all_to_all | solution.py:29
  28.8 7.7 %all-gather.gathered_ref = bf16[64,16,128]{2,1,0:T(8,128)(2,1)S(1)} all-gather(bf16[16,16,128]{2,1,0:T(8,128)(2,1)S(1)} %all-to-all-done), channel_id=2, replica_groups=mesh['section'=8,'x'=2,'z'=16,'c'=2] {'x','c'}, dimensions={0}, use_global_device_ids=true | all-gather | bytes 327680 | tf_op jit(solution)/shard_map/all_gather | solution.py:30
  36.5 0.9 shard_map.82
  37.5 0.7 constant_dynamic-update-slice_fusion
  38.1 4.5 %all-to-all-start.1 = ((bf16[64,7,4,128]{3,2,1,0:T(4,128)(2,1)}), bf16[64,7,4,128]{3,2,1,0:T(4,128)(2,1)S(1)}, u32[]{:S(2)}, u32[]{:S(2)}) async-start(bf16[64,7,4,128]{3,2,1,0:T(4,128)(2,1)} %constant_dynamic-update-slice_fusion), calls=%async_computation.1 | async-start | bytes 917504 | tf_op jit(solution)/shard_map/all_to_all | solution.py:150
  42.8 0.1 lt.99
  43.1 0.1 compare_and_fusion.3
  43.2 0.1 fusion.1.bias_ref
  43.3 28.8 %all-to-all-done.1 = bf16[64,7,4,128]{3,2,1,0:T(4,128)(2,1)S(1)} async-done(((bf16[64,7,4,128]{3,2,1,0:T(4,128)(2,1)}), bf16[64,7,4,128]{3,2,1,0:T(4,128)(2,1)S(1)}, u32[]{:S(2)}, u32[]{:S(2)}) %all-to-all-start.1) | async-done | bytes 458784 | tf_op jit(solution)/shard_map/all_to_all | solution.py:150
  72.2 0.7 shard_map.83
  72.9 15.1 %all_to_all.15 = bf16[16,16,128]{2,1,0:T(8,128)(2,1)S(1)} all-to-all(bf16[16,16,128]{2,1,0:T(8,128)(2,1)S(1)} %broadcast_in_dim.26), channel_id=1, replica_groups=mesh['section'=8,'x'=2,'z'=16,'c'=2] {'z'}, dimensions={0} | all-to-all | bytes 131072 | tf_op jit(solution)/shard_map/all_to_all | solution.py:29
  88.0 7.8 %all-gather.1 = bf16[64,16,128]{2,1,0:T(8,128)(2,1)S(1)} all-gather(bf16[16,16,128]{2,1,0:T(8,128)(2,1)S(1)} %all_to_all.15), channel_id=3, replica_groups=mesh['section'=8,'x'=2,'z'=16,'c'=2] {'x','c'}, dimensions={0}, use_global_device_ids=true | all-gather | bytes 327680 | tf_op jit(solution)/shard_map/all_gather | solution.py:30
  95.9 0.1 reshape.178.attn_ref
  96.1 0.4 shard_map.84
  96.5 3.2 %collective-permute-start = (bf16[16,128]{1,0:T(8,128)(2,1)S(1)}, bf16[16,128]{1,0:T(8,128)(2,1)S(1)}, u32[]{:S(2)}, u32[]{:S(2)}) collective-permute-start(bf16[16,128]{1,0:T(8,128)(2,1)S(1)} %shard_map.84), channel_id=1, source_target_pairs={{0,64},{64,128},{128,192},{192,256},{256,320},{320,384},{384,448},... | collective-permute-start | bytes 12296 | tf_op jit(solution)/shard_map/ppermute | solution.py:205
  99.7 4.8 %collective-permute-done = bf16[16,128]{1,0:T(8,128)(2,1)S(1)} collective-permute-done((bf16[16,128]{1,0:T(8,128)(2,1)S(1)}, bf16[16,128]{1,0:T(8,128)(2,1)S(1)}, u32[]{:S(2)}, u32[]{:S(2)}) %collective-permute-start) | collective-permute-done | bytes 4128 | tf_op jit(solution)/shard_map/ppermute | solution.py:205
  104.4 0.6 copy.17
  (32 shorter events, 0.6 us)
Async XLA Ops:
  0.0 42.7 %copy-start = (s32[1,16]{1,0:T(1,128)S(1)}, s32[1,16]{1,0:T(1,128)}, u32[]{:S(2)}) copy-start(s32[1,16]{1,0:T(1,128)} %param.14) | copy-start | bytes 196
  0.0 36.5 %copy-start.4 = (bf16[1,8192]{1,0:T(2,128)(2,1)S(1)}, bf16[1,8192]{1,0:T(2,128)(2,1)}, u32[]{:S(2)}) copy-start(bf16[1,8192]{1,0:T(2,128)(2,1)} %gain_ref.1) | copy-start | bytes 49156
  0.0 36.5 %copy-start.1 = (bf16[1,8192,128]{2,1,0:T(8,128)(2,1)S(1)}, bf16[1,8192,128]{2,1,0:T(8,128)(2,1)}, u32[]{:S(2)}) copy-start(bf16[1,8192,128]{2,1,0:T(8,128)(2,1)} %param.10) | copy-start | bytes 6291460
  0.0 36.5 %copy-start.3 = (bf16[1,8192,32]{1,2,0:T(8,128)(2,1)S(1)}, bf16[1,8192,32]{1,2,0:T(8,128)(2,1)}, u32[]{:S(2)}) copy-start(bf16[1,8192,32]{1,2,0:T(8,128)(2,1)} %param.11) | copy-start | bytes 1572868
  1.5 27.3 %all-to-all-start = ((bf16[16,16,128]{2,1,0:T(8,128)(2,1)}), bf16[16,16,128]{2,1,0:T(8,128)(2,1)S(1)}, u32[]{:S(2)}, u32[]{:S(2)}) async-start(bf16[16,16,128]{2,1,0:T(8,128)(2,1)} %broadcast_in_dim.19), calls=%async_computation | async-start | bytes 131072 | tf_op jit(solution)/shard_map/all_to_all | solution.py:29
  37.4 58.6 %copy-start.2 = (bf16[1,8192,128]{2,1,0:T(8,128)(2,1)S(1)}, bf16[1,8192,128]{2,1,0:T(8,128)(2,1)}, u32[]{:S(2)}) copy-start(bf16[1,8192,128]{2,1,0:T(8,128)(2,1)} %param.12) | copy-start | bytes 6291460
  37.4 58.6 %copy-start.5 = (bf16[1,16,128]{2,1,0:T(8,128)(2,1)S(1)}, bf16[1,16,128]{2,1,0:T(8,128)(2,1)}, u32[]{:S(2)}) copy-start(bf16[1,16,128]{2,1,0:T(8,128)(2,1)} %param.8) | copy-start | bytes 12292
  38.1 34.0 %all-to-all-start.1 = ((bf16[64,7,4,128]{3,2,1,0:T(4,128)(2,1)}), bf16[64,7,4,128]{3,2,1,0:T(4,128)(2,1)S(1)}, u32[]{:S(2)}, u32[]{:S(2)}) async-start(bf16[64,7,4,128]{3,2,1,0:T(4,128)(2,1)} %constant_dynamic-update-slice_fusion), calls=%async_computation.1 | async-start | bytes 917504 | tf_op jit(solution)/shard_map/all_to_all | solution.py:150
  96.5 8.0 %collective-permute-start = (bf16[16,128]{1,0:T(8,128)(2,1)S(1)}, bf16[16,128]{1,0:T(8,128)(2,1)S(1)}, u32[]{:S(2)}, u32[]{:S(2)}) collective-permute-start(bf16[16,128]{1,0:T(8,128)(2,1)S(1)} %shard_map.84), channel_id=1, source_target_pairs={{0,64},{64,128},{128,192},{192,256},{256,320},{320,384},{384,448},... | collective-permute-start | bytes 12296 | tf_op jit(solution)/shard_map/ppermute | solution.py:205

commit v5 on v4

--- a/solution.py
+++ b/solution.py
@@ -11,7 +11,8 @@
 
 HEAD_WIDTH = 128
 KEY_VALUE_HEADS = 8
-MINOR = ("x", "z", "c")
+LINE = ("za", "zb")
+MINOR = ("x",) + LINE + ("c",)
 
 
 def rotary_tables(token_positions):
@@ -24,15 +25,15 @@
 
 
 def spread(part):
-    line = lax.axis_size("z")
+    line = lax.axis_size(LINE)
     copies = jnp.broadcast_to(part[None], (line,) + part.shape)
-    along = lax.all_to_all(copies, "z", 0, 0)
+    along = lax.all_to_all(copies, LINE, 0, 0)
     full = lax.all_gather(along, ("x", "c"))
     return full.reshape((lax.axis_size("x"), lax.axis_size("c"), line) + part.shape)
 
 
 def place_rows(cores, line, gathered_ref, gain_ref, query_ref, keyval_ref, cosine_ref, sine_ref,
-               share_ref, out_ref, normed_ref):
+               share_ref, out_ref, near_ref, normed_ref):
     rows, width = gathered_ref.shape[1:]
     squares = jnp.zeros((rows, width), jnp.float32)
     for at in range(gathered_ref.shape[0]):
@@ -56,20 +57,18 @@
     lane = lax.broadcasted_iota(jnp.int32, (part, width), 1)
     column = lax.broadcasted_iota(jnp.int32, (part, width), 0)
     place = jnp.where(lane == column + share_ref[0] * part, 1.0, 0.0).astype(jnp.bfloat16)
-    placed = jnp.dot(keyval, place, preferred_element_type=jnp.float32).astype(jnp.bfloat16)
-    both = jnp.concatenate([query.astype(jnp.bfloat16), placed], axis=0)
-    to = lax.broadcasted_iota(jnp.int32, (2 * rows, 2 * rows), 0)
-    source = lax.broadcasted_iota(jnp.int32, (2 * rows, 2 * rows), 1)
-    wanted = (to // 4) * 2 + to % 2 + jnp.where(to % 4 >= 2, rows, 0)
-    order = jnp.where(source == wanted, 1.0, 0.0).astype(jnp.bfloat16)
-    out_ref[...] = jnp.dot(order, both, preferred_element_type=jnp.float32).astype(jnp.bfloat16)
-
-
-def attend(span, factor, entries_ref, select_ref, bias_ref, cosine_ref, sine_ref, out_ref):
+    placed = jnp.dot(keyval, place, preferred_element_type=jnp.float32)
+    near_ref[...] = placed.astype(jnp.bfloat16)
+    out_ref[...] = query.astype(jnp.bfloat16)
+
+
+def attend(span, factor, entries_ref, near_ref, select_ref, near_select_ref, bias_ref, cosine_ref,
+           sine_ref, out_ref):
     entries = entries_ref[...]
     rows, width = out_ref.shape
     picked = jnp.dot(select_ref[...], entries, preferred_element_type=jnp.float32)
-    query, fresh_key, fresh_value = picked[:rows], picked[rows : 2 * rows], picked[2 * rows :]
+    query = jnp.dot(near_select_ref[...], near_ref[...], preferred_element_type=jnp.float32)
+    fresh_key, fresh_value = picked[:rows], picked[rows:]
     scores = lax.dot_general(
         query.astype(jnp.bfloat16),
         entries,
@@ -106,7 +105,7 @@
     positions,
 ):
     rows = resid.shape[1]
-    devices = lax.axis_size("x") * lax.axis_size("z") * lax.axis_size("c")
+    devices = lax.axis_size(MINOR)
     groups = KEY_VALUE_HEADS
     members = devices // groups
     own_rows = rows // members
@@ -116,7 +115,7 @@
 
     pieces = key_value_cache[0].reshape(members, own_rows, span, 2, groups, HEAD_WIDTH)
     pieces = pieces.transpose(4, 0, 3, 2, 1, 5).reshape(
-        devices, span, 2 * own_rows, HEAD_WIDTH
+        devices, 2 * span, own_rows, HEAD_WIDTH
     )
     pieces = lax.optimization_barrier(jnp.pad(pieces, ((0, 0), (0, 1), (0, 0), (0, 0))))
 
@@ -126,11 +125,14 @@
     width = key_value_weight.shape[2]
     shares = HEAD_WIDTH // width
     whole, small = pl.BlockSpec(memory_space=pltpu.VMEM), pl.BlockSpec(memory_space=pltpu.SMEM)
-    own = pl.pallas_call(
+    query, fresh = pl.pallas_call(
         functools.partial(place_rows, cores, line),
-        out_shape=jax.ShapeDtypeStruct((2 * rows, HEAD_WIDTH), jnp.bfloat16),
+        out_shape=(
+            jax.ShapeDtypeStruct((rows, HEAD_WIDTH), jnp.bfloat16),
+            jax.ShapeDtypeStruct((rows, HEAD_WIDTH), jnp.bfloat16),
+        ),
         in_specs=[whole] * 6 + [small],
-        out_specs=whole,
+        out_specs=(whole, whole),
         scratch_shapes=[pltpu.VMEM((rows, query_weight.shape[1]), jnp.bfloat16)],
         compiler_params=pltpu.CompilerParams(vmem_limit_bytes=24 * 2**20),
     )(
@@ -142,12 +144,17 @@
         jnp.concatenate([-sine, sine], axis=1),
         (me % shares).reshape(1),
     )
-    own = own.reshape(members, 2 * own_rows, HEAD_WIDTH)
-    own = jnp.broadcast_to(own[None], (groups,) + own.shape).reshape(
-        devices, 1, 2 * own_rows, HEAD_WIDTH
-    )
-    sent = lax.dynamic_update_slice_in_dim(pieces, own, pieces.shape[1] - 1, axis=1)
+    fresh = jnp.broadcast_to(fresh[None], (groups,) + fresh.shape)
+    fresh = fresh.reshape(devices, 1, own_rows, HEAD_WIDTH)
+    sent = lax.dynamic_update_slice_in_dim(pieces, fresh, pieces.shape[1] - 1, axis=1)
     arrived = lax.all_to_all(sent, MINOR, 0, 0).reshape(devices, -1, HEAD_WIDTH)
+    chip = lax.all_gather(query, "c")
+    chips = lax.axis_size("zb")
+    near = [chip] + [
+        lax.ppermute(chip, "zb", [(i, (i + by) % chips) for i in range(chips)])
+        for by in range(1, chips)
+    ]
+    near = jnp.stack(near).reshape(members * rows, HEAD_WIDTH)
     per_device = arrived.shape[1]
     cached = 2 * span * own_rows
     entries = devices * per_device
@@ -161,28 +168,36 @@
     entry_slot = entry_from * span + entry_at // own_rows
     rank = jnp.arange(members * own_rows, dtype=jnp.int32)[:, None]
     rank_row = rank % own_rows
-    is_query = (entry_at >= cached) & (entry_at < cached + own_rows)
-    is_fresh = entry_at >= cached + own_rows
-    select = [
-        is_query & (entry_from == group * members + rank // own_rows),
-        is_fresh & (entry_from // shares == group),
-        is_fresh & (entry_from // shares == groups + group),
-    ]
-    select = jnp.concatenate([part & (entry_row == rank_row) for part in select]).astype(
-        jnp.bfloat16
-    )
+    holders = [group * shares, devices // 2 + group * shares]
+    select = jnp.concatenate(
+        [
+            (entry_at >= cached) & (entry_from // shares == holder // shares)
+            & (entry_row == rank_row)
+            for holder in holders
+        ]
+    ).astype(jnp.bfloat16)
+    near_at = jnp.arange(members * rows, dtype=jnp.int32)
+    per_chip = rows * members // chips
+    near_chip = (lax.axis_index("zb") - near_at // per_chip) % chips
+    near_from = near_chip * (members // chips) + near_at % per_chip // rows
+    near_select = (near_from == rank // own_rows) & (
+        near_at % rows == member * own_rows + rank_row
+    )
+    near_select = near_select.astype(jnp.bfloat16)
     live = (entry_at < span * own_rows) & (entry_row == rank_row)
     live = live & (entry_slot < jnp.tile(own_lengths, members)[:, None])
     bias = jnp.where(live, 0.0, -1e30)
     attn = pl.pallas_call(
         functools.partial(attend, span * own_rows, 1.0 / math.sqrt(HEAD_WIDTH)),
         out_shape=jax.ShapeDtypeStruct((members * own_rows, HEAD_WIDTH), jnp.bfloat16),
-        in_specs=[whole] * 5,
+        in_specs=[whole] * 7,
         out_specs=whole,
         compiler_params=pltpu.CompilerParams(vmem_limit_bytes=24 * 2**20),
     )(
         arrived.reshape(entries, HEAD_WIDTH),
+        near,
         select,
+        near_select,
         bias,
         jnp.tile(jnp.concatenate([own_cosine, own_cosine], axis=1), (members, 1)),
         jnp.tile(jnp.concatenate([-own_sine, own_sine], axis=1), (members, 1)),
@@ -207,9 +222,9 @@
 
 def solution(mesh):
     sections, devices = mesh.devices.shape
-    chips = devices // 4
+    near = devices // KEY_VALUE_HEADS // 2
     split = Mesh(
-        mesh.devices.reshape(sections, 2, chips, 2), ("section",) + MINOR
+        mesh.devices.reshape(sections, 2, devices // (4 * near), near, 2), ("section",) + MINOR
     )
     return jax.shard_map(
         body,

time: 105 us -> 104 us (level)
  waiting for transfers between devices: 41.8 us -> 28.9 us
  starting transfers between devices: 23.5 us -> 33 us
  blocking collectives: 30.6 us -> 33 us
    all_to_all x1, waiting for transfers between devices: 28.8 us -> 9.04 us  [body(): arrived = lax.all_to_all(sent, MINOR, 0, 0).reshape(devices, -1, HEAD_WIDTH)]
    ppermute x0 -> x3, starting transfers between devices: none -> 9.37 us  [body(): lax.ppermute(chip, 'zb', [(i, (i + by) % chips) for i in range(chips)])]
    ppermute x0 -> x3, waiting for transfers between devices: none -> 7.26 us  [body(): lax.ppermute(chip, 'zb', [(i, (i + by) % chips) for i in range(chips)])]
    all_gather x0 -> x1, blocking collectives: none -> 1.95 us  [body(): chip = lax.all_gather(query, 'c')]
  transfers between devices with their start and end apart: 3 -> 6, of which waited for: 3 -> 5; matrix products, arithmetic and copies ran while one was open for 4% -> 4% of each run, Pallas kernels for 0% -> 0%
where the time goes in v5:
time: 104 us
  starting transfers between devices  33 us (32%)
  blocking collectives  33 us (32%)
  waiting for transfers between devices  28.9 us (28%)
  local copies, waits for them, and re-layouts  5.52 us (5%)
  Pallas kernels  1.88 us (2%)
  other arithmetic  1.4 us (1%)
    all_to_all x1, starting transfers between devices, spread(): along = lax.all_to_all(copies, LINE, 0, 0)  15.7 us
    all_gather x2, blocking collectives, spread(): full = lax.all_gather(along, ('x', 'c'))  15.5 us
    all_to_all x1, blocking collectives, spread(): along = lax.all_to_all(copies, LINE, 0, 0)  15.5 us
    ppermute x3, starting transfers between devices, body(): lax.ppermute(chip, 'zb', [(i, (i + by) % chips) for i in range(chips)])  9.37 us
    all_to_all x1, waiting for transfers between devices, body(): arrived = lax.all_to_all(sent, MINOR, 0, 0).reshape(devices, -1, HEAD_WIDTH)  9.04 us
    all_to_all x1, waiting for transfers between devices, spread(): along = lax.all_to_all(copies, LINE, 0, 0)  7.83 us
    ppermute x3, waiting for transfers between devices, body(): lax.ppermute(chip, 'zb', [(i, (i + by) % chips) for i in range(chips)])  7.26 us
    ppermute x1, waiting for transfers between devices, body(): return lax.ppermute(updated, 'section', following)[None]  4.75 us
  transfers between devices with their start and end apart: 6, of which 5 were waited for; matrix products, arithmetic and copies ran while one was open for 4% of the time, Pallas kernels for 0%

profile of v5, /device:TPU:1, one launch (start us, length us, event | category | flops | bytes accessed | tf_op | source)
XLA Modules:
  0.0 104.0 jit_solution(7480949052632405953)
XLA Ops:
  0.0 1.5 %broadcast_in_dim.17 = bf16[16,16,128]{2,1,0:T(8,128)(2,1)} broadcast(bf16[16,128]{1,0:T(8,128)(2,1)} %bitcast.44), dimensions={1,2} | broadcast | bytes 69632 | tf_op jit(solution)/shard_map/broadcast_in_dim | solution.py:29
  1.5 15.7 %all-to-all-start = ((bf16[16,16,128]{2,1,0:T(8,128)(2,1)}), bf16[16,16,128]{2,1,0:T(8,128)(2,1)S(1)}, u32[]{:S(2)}, u32[]{:S(2)}) async-start(bf16[16,16,128]{2,1,0:T(8,128)(2,1)} %broadcast_in_dim.17), calls=%async_computation | async-start | bytes 131072 | tf_op jit(solution)/shard_map/all_to_all | solution.py:30
  17.4 0.7 convert_bitcast_fusion
  18.4 1.1 %copy.14 = bf16[12,8,16,128]{3,2,1,0:T(8,128)(2,1)S(1)} copy(bf16[12,8,16,128]{3,1,2,0:T(8,128)(2,1)} %bitcast.49) | data formatting | bytes 786432
  19.7 1.1 %pad.4 = bf16[64,13,2,128]{3,2,1,0:T(2,128)(2,1)} pad(bf16[64,12,2,128]{3,2,1,0:T(2,128)(2,1)S(1)} %bitcast.46, bf16[]{:T(256)} %constant.179.clone.1), padding=0_0x0_1x0_0x0_0 | pad | bytes 819202 | tf_op jit(solution)/shard_map/jit(_pad)/pad | solution.py:120
  21.0 7.8 %all-to-all-done = bf16[16,16,128]{2,1,0:T(8,128)(2,1)S(1)} async-done(((bf16[16,16,128]{2,1,0:T(8,128)(2,1)}), bf16[16,16,128]{2,1,0:T(8,128)(2,1)S(1)}, u32[]{:S(2)}, u32[]{:S(2)}) %all-to-all-start) | async-done | bytes 65568 | tf_op jit(solution)/shard_map/all_to_all | solution.py:30
  28.8 7.7 %all-gather.gathered_ref = bf16[64,16,128]{2,1,0:T(8,128)(2,1)S(1)} all-gather(bf16[16,16,128]{2,1,0:T(8,128)(2,1)S(1)} %all-to-all-done), channel_id=2, replica_groups=mesh['section'=8,'x'=2,'za'=4,'zb'=4,'c'=2] {'x','c'}, dimensions={0}, use_global_device_ids=true | all-gather | bytes 327680 | tf_op jit(solution)/shard_map/all_gather | solution.py:31
  36.5 0.8 shard_map.82
  37.3 0.6 constant_dynamic-update-slice_fusion
  38.0 4.7 %all-to-all-start.1 = ((bf16[64,13,2,128]{3,2,1,0:T(2,128)(2,1)}), bf16[64,13,2,128]{3,2,1,0:T(2,128)(2,1)S(1)}, u32[]{:S(2)}, u32[]{:S(2)}) async-start(bf16[64,13,2,128]{3,2,1,0:T(2,128)(2,1)} %constant_dynamic-update-slice_fusion), calls=%async_computation.1 | async-start | bytes 851968 | tf_op jit(solution)/shard_map/all_to_all | solution.py:150
  43.0 1.9 %all-gather.1 = bf16[32,128]{1,0:T(8,128)(2,1)S(1)} all-gather(bf16[16,128]{1,0:T(8,128)(2,1)S(1)} %get-tuple-element.8), channel_id=3, replica_groups=mesh['section'=8,'x'=2,'za'=4,'zb'=4,'c'=2] {'c'}, dimensions={0}, use_global_device_ids=true | all-gather | bytes 12288 | tf_op jit(solution)/shard_map/all_gather | solution.py:151
  45.0 5.0 %collective-permute-start.2 = (bf16[2,16,128]{2,1,0:T(8,128)(2,1)S(1)}, bf16[2,16,128]{2,1,0:T(8,128)(2,1)S(1)}, u32[]{:S(2)}, u32[]{:S(2)}) collective-permute-start(bf16[2,16,128]{2,1,0:T(8,128)(2,1)S(1)} %bitcast.51), channel_id=1, source_target_pairs={{0,6},{2,0},{4,2},{6,4},{1,7},{3,1},{5,3},{7,5},{8,14},{10,8},{12,... | collective-permute-start | bytes 24584 | tf_op jit(solution)/shard_map/ppermute | solution.py:154
  49.9 1.9 %collective-permute-start.1 = (bf16[2,16,128]{2,1,0:T(8,128)(2,1)S(1)}, bf16[2,16,128]{2,1,0:T(8,128)(2,1)S(1)}, u32[]{:S(2)}, u32[]{:S(2)}) collective-permute-start(bf16[2,16,128]{2,1,0:T(8,128)(2,1)S(1)} %bitcast.52), channel_id=1, source_target_pairs={{0,4},{2,6},{4,0},{6,2},{1,5},{3,7},{5,1},{7,3},{8,12},{10,14},{12... | collective-permute-start | bytes 24584 | tf_op jit(solution)/shard_map/ppermute | solution.py:154
  51.9 2.5 %collective-permute-start = (bf16[2,16,128]{2,1,0:T(8,128)(2,1)S(1)}, bf16[2,16,128]{2,1,0:T(8,128)(2,1)S(1)}, u32[]{:S(2)}, u32[]{:S(2)}) collective-permute-start(bf16[2,16,128]{2,1,0:T(8,128)(2,1)S(1)} %bitcast.53), channel_id=1, source_target_pairs={{0,2},{2,4},{4,6},{6,0},{1,3},{3,5},{5,7},{7,1},{8,10},{10,12},{12... | collective-permute-start | bytes 24584 | tf_op jit(solution)/shard_map/ppermute | solution.py:154
  54.4 6.6 %collective-permute-done.2 = bf16[2,16,128]{2,1,0:T(8,128)(2,1)S(1)} collective-permute-done((bf16[2,16,128]{2,1,0:T(8,128)(2,1)S(1)}, bf16[2,16,128]{2,1,0:T(8,128)(2,1)S(1)}, u32[]{:S(2)}, u32[]{:S(2)}) %collective-permute-start.2) | collective-permute-done | bytes 8224 | tf_op jit(solution)/shard_map/ppermute | solution.py:154
  61.1 0.6 collective-permute-done.1
  61.7 9.0 %all-to-all-done.1 = bf16[64,13,2,128]{3,2,1,0:T(2,128)(2,1)S(1)} async-done(((bf16[64,13,2,128]{3,2,1,0:T(2,128)(2,1)}), bf16[64,13,2,128]{3,2,1,0:T(2,128)(2,1)S(1)}, u32[]{:S(2)}, u32[]{:S(2)}) %all-to-all-start.1) | async-done | bytes 426016 | tf_op jit(solution)/shard_map/all_to_all | solution.py:150
  70.7 0.7 shard_map.83
  71.5 15.5 %all_to_all.15 = bf16[16,16,128]{2,1,0:T(8,128)(2,1)S(1)} all-to-all(bf16[16,16,128]{2,1,0:T(8,128)(2,1)S(1)} %broadcast_in_dim.23), channel_id=1, replica_groups=mesh['section'=8,'x'=2,'za'=4,'zb'=4,'c'=2] {'za','zb'}, dimensions={0} | all-to-all | bytes 131072 | tf_op jit(solution)/shard_map/all_to_all | solution.py:30
  87.0 7.8 %all-gather.2 = bf16[64,16,128]{2,1,0:T(8,128)(2,1)S(1)} all-gather(bf16[16,16,128]{2,1,0:T(8,128)(2,1)S(1)} %all_to_all.15), channel_id=4, replica_groups=mesh['section'=8,'x'=2,'za'=4,'zb'=4,'c'=2] {'x','c'}, dimensions={0}, use_global_device_ids=true | all-gather | bytes 327680 | tf_op jit(solution)/shard_map/all_gather | solution.py:31
  95.0 0.4 shard_map.84
  95.4 3.2 %collective-permute-start.3 = (bf16[16,128]{1,0:T(8,128)(2,1)S(1)}, bf16[16,128]{1,0:T(8,128)(2,1)S(1)}, u32[]{:S(2)}, u32[]{:S(2)}) collective-permute-start(bf16[16,128]{1,0:T(8,128)(2,1)S(1)} %shard_map.84), channel_id=1, source_target_pairs={{0,64},{64,128},{128,192},{192,256},{256,320},{320,384},{384,448},... | collective-permute-start | bytes 12296 | tf_op jit(solution)/shard_map/ppermute | solution.py:220
  98.6 4.8 %collective-permute-done.3 = bf16[16,128]{1,0:T(8,128)(2,1)S(1)} collective-permute-done((bf16[16,128]{1,0:T(8,128)(2,1)S(1)}, bf16[16,128]{1,0:T(8,128)(2,1)S(1)}, u32[]{:S(2)}, u32[]{:S(2)}) %collective-permute-start.3) | collective-permute-done | bytes 4128 | tf_op jit(solution)/shard_map/ppermute | solution.py:220
  103.4 0.6 copy.17
  (40 shorter events, 1.4 us)
Async XLA Ops:
  0.0 18.3 %copy-start = (s32[1,16]{1,0:T(1,128)S(1)}, s32[1,16]{1,0:T(1,128)}, u32[]{:S(2)}) copy-start(s32[1,16]{1,0:T(1,128)} %param.14) | copy-start | bytes 196
  0.0 36.5 %copy-start.4 = (bf16[1,8192]{1,0:T(2,128)(2,1)S(1)}, bf16[1,8192]{1,0:T(2,128)(2,1)}, u32[]{:S(2)}) copy-start(bf16[1,8192]{1,0:T(2,128)(2,1)} %gain_ref.1) | copy-start | bytes 49156
  0.0 36.5 %copy-start.1 = (bf16[1,8192,128]{2,1,0:T(8,128)(2,1)S(1)}, bf16[1,8192,128]{2,1,0:T(8,128)(2,1)}, u32[]{:S(2)}) copy-start(bf16[1,8192,128]{2,1,0:T(8,128)(2,1)} %param.10) | copy-start | bytes 6291460
  0.0 36.5 %copy-start.3 = (bf16[1,8192,32]{1,2,0:T(8,128)(2,1)S(1)}, bf16[1,8192,32]{1,2,0:T(8,128)(2,1)}, u32[]{:S(2)}) copy-start(bf16[1,8192,32]{1,2,0:T(8,128)(2,1)} %param.11) | copy-start | bytes 1572868
  1.5 27.3 %all-to-all-start = ((bf16[16,16,128]{2,1,0:T(8,128)(2,1)}), bf16[16,16,128]{2,1,0:T(8,128)(2,1)S(1)}, u32[]{:S(2)}, u32[]{:S(2)}) async-start(bf16[16,16,128]{2,1,0:T(8,128)(2,1)} %broadcast_in_dim.17), calls=%async_computation | async-start | bytes 131072 | tf_op jit(solution)/shard_map/all_to_all | solution.py:30
  37.3 57.7 %copy-start.2 = (bf16[1,8192,128]{2,1,0:T(8,128)(2,1)S(1)}, bf16[1,8192,128]{2,1,0:T(8,128)(2,1)}, u32[]{:S(2)}) copy-start(bf16[1,8192,128]{2,1,0:T(8,128)(2,1)} %param.12) | copy-start | bytes 6291460
  37.3 57.7 %copy-start.5 = (bf16[1,16,128]{2,1,0:T(8,128)(2,1)S(1)}, bf16[1,16,128]{2,1,0:T(8,128)(2,1)}, u32[]{:S(2)}) copy-start(bf16[1,16,128]{2,1,0:T(8,128)(2,1)} %param.8) | copy-start | bytes 12292
  38.0 32.8 %all-to-all-start.1 = ((bf16[64,13,2,128]{3,2,1,0:T(2,128)(2,1)}), bf16[64,13,2,128]{3,2,1,0:T(2,128)(2,1)S(1)}, u32[]{:S(2)}, u32[]{:S(2)}) async-start(bf16[64,13,2,128]{3,2,1,0:T(2,128)(2,1)} %constant_dynamic-update-slice_fusion), calls=%async_computation.1 | async-start | bytes 851968 | tf_op jit(solution)/shard_map/all_to_all | solution.py:150
  45.0 16.1 %collective-permute-start.2 = (bf16[2,16,128]{2,1,0:T(8,128)(2,1)S(1)}, bf16[2,16,128]{2,1,0:T(8,128)(2,1)S(1)}, u32[]{:S(2)}, u32[]{:S(2)}) collective-permute-start(bf16[2,16,128]{2,1,0:T(8,128)(2,1)S(1)} %bitcast.51), channel_id=1, source_target_pairs={{0,6},{2,0},{4,2},{6,4},{1,7},{3,1},{5,3},{7,5},{8,14},{10,8},{12,... | collective-permute-start | bytes 24584 | tf_op jit(solution)/shard_map/ppermute | solution.py:154
  49.9 11.7 %collective-permute-start.1 = (bf16[2,16,128]{2,1,0:T(8,128)(2,1)S(1)}, bf16[2,16,128]{2,1,0:T(8,128)(2,1)S(1)}, u32[]{:S(2)}, u32[]{:S(2)}) collective-permute-start(bf16[2,16,128]{2,1,0:T(8,128)(2,1)S(1)} %bitcast.52), channel_id=1, source_target_pairs={{0,4},{2,6},{4,0},{6,2},{1,5},{3,7},{5,1},{7,3},{8,12},{10,14},{12... | collective-permute-start | bytes 24584 | tf_op jit(solution)/shard_map/ppermute | solution.py:154
  51.9 9.8 %collective-permute-start = (bf16[2,16,128]{2,1,0:T(8,128)(2,1)S(1)}, bf16[2,16,128]{2,1,0:T(8,128)(2,1)S(1)}, u32[]{:S(2)}, u32[]{:S(2)}) collective-permute-start(bf16[2,16,128]{2,1,0:T(8,128)(2,1)S(1)} %bitcast.53), channel_id=1, source_target_pairs={{0,2},{2,4},{4,6},{6,0},{1,3},{3,5},{5,7},{7,1},{8,10},{10,12},{12... | collective-permute-start | bytes 24584 | tf_op jit(solution)/shard_map/ppermute | solution.py:154
  95.4 8.0 %collective-permute-start.3 = (bf16[16,128]{1,0:T(8,128)(2,1)S(1)}, bf16[16,128]{1,0:T(8,128)(2,1)S(1)}, u32[]{:S(2)}, u32[]{:S(2)}) collective-permute-start(bf16[16,128]{1,0:T(8,128)(2,1)S(1)} %shard_map.84), channel_id=1, source_target_pairs={{0,64},{64,128},{128,192},{192,256},{256,320},{320,384},{384,448},... | collective-permute-start | bytes 12296 | tf_op jit(solution)/shard_map/ppermute | solution.py:220

commit v6 on v5

--- a/solution.py
+++ b/solution.py
@@ -32,8 +32,7 @@
     return full.reshape((lax.axis_size("x"), lax.axis_size("c"), line) + part.shape)
 
 
-def place_rows(cores, line, gathered_ref, gain_ref, query_ref, keyval_ref, cosine_ref, sine_ref,
-               share_ref, out_ref, near_ref, normed_ref):
+def place_rows(cores, line, gathered_ref, gain_ref, keyval_ref, share_ref, fresh_ref, normed_ref):
     rows, width = gathered_ref.shape[1:]
     squares = jnp.zeros((rows, width), jnp.float32)
     for at in range(gathered_ref.shape[0]):
@@ -47,18 +46,24 @@
         gain = gain_ref[:, first : first + width].astype(jnp.float32)
         wide = gathered_ref[at].astype(jnp.float32)
         normed_ref[:, first : first + width] = (wide * scale * gain).astype(jnp.bfloat16)
-    normed = normed_ref[...]
-    query = jnp.dot(normed, query_ref[...], preferred_element_type=jnp.float32)
     keyval = lax.dot_general(
-        normed, keyval_ref[...], (((1,), (1,)), ((), ())), preferred_element_type=jnp.float32
+        normed_ref[...],
+        keyval_ref[...],
+        (((1,), (1,)), ((), ())),
+        preferred_element_type=jnp.float32,
     ).astype(jnp.bfloat16)
-    query = query * cosine_ref[...] + pltpu.roll(query, width // 2, 1) * sine_ref[...]
     part = keyval.shape[1]
     lane = lax.broadcasted_iota(jnp.int32, (part, width), 1)
     column = lax.broadcasted_iota(jnp.int32, (part, width), 0)
     place = jnp.where(lane == column + share_ref[0] * part, 1.0, 0.0).astype(jnp.bfloat16)
     placed = jnp.dot(keyval, place, preferred_element_type=jnp.float32)
-    near_ref[...] = placed.astype(jnp.bfloat16)
+    fresh_ref[...] = placed.astype(jnp.bfloat16)
+
+
+def rotate_query(normed_ref, query_ref, cosine_ref, sine_ref, out_ref):
+    query = jnp.dot(normed_ref[...], query_ref[...], preferred_element_type=jnp.float32)
+    turned = pltpu.roll(query, query.shape[1] // 2, 1)
+    query = query * cosine_ref[...] + turned * sine_ref[...]
     out_ref[...] = query.astype(jnp.bfloat16)
 
 
@@ -125,24 +130,32 @@
     width = key_value_weight.shape[2]
     shares = HEAD_WIDTH // width
     whole, small = pl.BlockSpec(memory_space=pltpu.VMEM), pl.BlockSpec(memory_space=pltpu.SMEM)
-    query, fresh = pl.pallas_call(
+    fresh, normed = pl.pallas_call(
         functools.partial(place_rows, cores, line),
         out_shape=(
             jax.ShapeDtypeStruct((rows, HEAD_WIDTH), jnp.bfloat16),
-            jax.ShapeDtypeStruct((rows, HEAD_WIDTH), jnp.bfloat16),
+            jax.ShapeDtypeStruct((rows, query_weight.shape[1]), jnp.bfloat16),
         ),
-        in_specs=[whole] * 6 + [small],
+        in_specs=[whole] * 3 + [small],
         out_specs=(whole, whole),
-        scratch_shapes=[pltpu.VMEM((rows, query_weight.shape[1]), jnp.bfloat16)],
         compiler_params=pltpu.CompilerParams(vmem_limit_bytes=24 * 2**20),
     )(
         gathered.reshape((devices,) + resid.shape[1:]),
         norm_gain,
+        key_value_weight[0].T,
+        (me % shares).reshape(1),
+    )
+    query = pl.pallas_call(
+        rotate_query,
+        out_shape=jax.ShapeDtypeStruct((rows, HEAD_WIDTH), jnp.bfloat16),
+        in_specs=[whole] * 4,
+        out_specs=whole,
+        compiler_params=pltpu.CompilerParams(vmem_limit_bytes=24 * 2**20),
+    )(
+        normed,
         query_weight[0],
-        key_value_weight[0].T,
         jnp.concatenate([cosine, cosine], axis=1),
         jnp.concatenate([-sine, sine], axis=1),
-        (me % shares).reshape(1),
     )
     fresh = jnp.broadcast_to(fresh[None], (groups,) + fresh.shape)
     fresh = fresh.reshape(devices, 1, own_rows, HEAD_WIDTH)

time: 104 us -> 104 us (level)
  waiting for transfers between devices: 28.9 us -> 27.3 us
    ppermute x3, waiting for transfers between devices: 7.26 us -> 5.27 us  [body(): lax.ppermute(chip, 'zb', [(i, (i + by) % chips) for i in range(chips)])]
  transfers between devices with their start and end apart: 6 -> 6, of which waited for: 5 -> 6; matrix products, arithmetic and copies ran while one was open for 4% -> 4% of each run, Pallas kernels for 0% -> 0%
where the time goes in v6:
time: 104 us; the launch traced here: 103 us
  starting transfers between devices  33.8 us (32%)
  blocking collectives  33 us (32%)
  waiting for transfers between devices  27.3 us (26%)
  local copies, waits for them, and re-layouts  5.43 us (5%)
  Pallas kernels  2.08 us (2%)
  other arithmetic  1.4 us (1%)
    all_to_all x1, starting transfers between devices, spread(): along = lax.all_to_all(copies, LINE, 0, 0)  15.7 us
    all_gather x2, blocking collectives, spread(): full = lax.all_gather(along, ('x', 'c'))  15.5 us
    all_to_all x1, blocking collectives, spread(): along = lax.all_to_all(copies, LINE, 0, 0)  15.4 us
    ppermute x3, starting transfers between devices, body(): lax.ppermute(chip, 'zb', [(i, (i + by) % chips) for i in range(chips)])  10.3 us
    all_to_all x1, waiting for transfers between devices, body(): arrived = lax.all_to_all(sent, MINOR, 0, 0).reshape(devices, -1, HEAD_WIDTH)  9.52 us
    all_to_all x1, waiting for transfers between devices, spread(): along = lax.all_to_all(copies, LINE, 0, 0)  7.77 us
    ppermute x3, waiting for transfers between devices, body(): lax.ppermute(chip, 'zb', [(i, (i + by) % chips) for i in range(chips)])  5.27 us
    ppermute x1, waiting for transfers between devices, body(): return lax.ppermute(updated, 'section', following)[None]  4.75 us
  transfers between devices with their start and end apart: 6, of which 6 were waited for; matrix products, arithmetic and copies ran while one was open for 4% of the time, Pallas kernels for 0%

profile of v6, /device:TPU:1, one launch (start us, length us, event | category | flops | bytes accessed | tf_op | source)
XLA Modules:
  0.0 103.3 jit_solution(14049623511278037951)
XLA Ops:
  0.0 1.4 %broadcast_in_dim.17 = bf16[16,16,128]{2,1,0:T(8,128)(2,1)} broadcast(bf16[16,128]{1,0:T(8,128)(2,1)} %bitcast.44), dimensions={1,2} | broadcast | bytes 69632 | tf_op jit(solution)/shard_map/broadcast_in_dim | solution.py:29
  1.4 15.7 %all-to-all-start = ((bf16[16,16,128]{2,1,0:T(8,128)(2,1)}), bf16[16,16,128]{2,1,0:T(8,128)(2,1)S(1)}, u32[]{:S(2)}, u32[]{:S(2)}) async-start(bf16[16,16,128]{2,1,0:T(8,128)(2,1)} %broadcast_in_dim.17), calls=%async_computation | async-start | bytes 131072 | tf_op jit(solution)/shard_map/all_to_all | solution.py:30
  17.3 0.7 convert_bitcast_fusion
  18.3 1.1 %copy.14 = bf16[12,8,16,128]{3,2,1,0:T(8,128)(2,1)S(1)} copy(bf16[12,8,16,128]{3,1,2,0:T(8,128)(2,1)} %bitcast.49) | data formatting | bytes 786432
  19.7 1.1 %pad.4 = bf16[64,13,2,128]{3,2,1,0:T(2,128)(2,1)} pad(bf16[64,12,2,128]{3,2,1,0:T(2,128)(2,1)S(1)} %bitcast.46, bf16[]{:T(256)} %constant.179.clone.1), padding=0_0x0_1x0_0x0_0 | pad | bytes 819202 | tf_op jit(solution)/shard_map/jit(_pad)/pad | solution.py:125
  20.9 7.8 %all-to-all-done = bf16[16,16,128]{2,1,0:T(8,128)(2,1)S(1)} async-done(((bf16[16,16,128]{2,1,0:T(8,128)(2,1)}), bf16[16,16,128]{2,1,0:T(8,128)(2,1)S(1)}, u32[]{:S(2)}, u32[]{:S(2)}) %all-to-all-start) | async-done | bytes 65568 | tf_op jit(solution)/shard_map/all_to_all | solution.py:30
  28.7 7.7 %all-gather.gathered_ref = bf16[64,16,128]{2,1,0:T(8,128)(2,1)S(1)} all-gather(bf16[16,16,128]{2,1,0:T(8,128)(2,1)S(1)} %all-to-all-done), channel_id=2, replica_groups=mesh['section'=8,'x'=2,'za'=4,'zb'=4,'c'=2] {'x','c'}, dimensions={0}, use_global_device_ids=true | all-gather | bytes 327680 | tf_op jit(solution)/shard_map/all_gather | solution.py:31
  36.4 0.5 shard_map.82
  37.0 0.6 constant_dynamic-update-slice_fusion
  37.6 4.6 %all-to-all-start.1 = ((bf16[64,13,2,128]{3,2,1,0:T(2,128)(2,1)}), bf16[64,13,2,128]{3,2,1,0:T(2,128)(2,1)S(1)}, u32[]{:S(2)}, u32[]{:S(2)}) async-start(bf16[64,13,2,128]{3,2,1,0:T(2,128)(2,1)} %constant_dynamic-update-slice_fusion), calls=%async_computation.1 | async-start | bytes 851968 | tf_op jit(solution)/shard_map/all_to_all | solution.py:163
  42.5 0.5 shard_map.83
  43.0 2.1 %all-gather.1 = bf16[32,128]{1,0:T(8,128)(2,1)S(1)} all-gather(bf16[16,128]{1,0:T(8,128)(2,1)S(1)} %shard_map.83), channel_id=3, replica_groups=mesh['section'=8,'x'=2,'za'=4,'zb'=4,'c'=2] {'c'}, dimensions={0}, use_global_device_ids=true | all-gather | bytes 12288 | tf_op jit(solution)/shard_map/all_gather | solution.py:164
  45.1 3.2 %collective-permute-start = (bf16[2,16,128]{2,1,0:T(8,128)(2,1)S(1)}, bf16[2,16,128]{2,1,0:T(8,128)(2,1)S(1)}, u32[]{:S(2)}, u32[]{:S(2)}) collective-permute-start(bf16[2,16,128]{2,1,0:T(8,128)(2,1)S(1)} %bitcast.51), channel_id=1, source_target_pairs={{0,2},{2,4},{4,6},{6,0},{1,3},{3,5},{5,7},{7,1},{8,10},{10,12},{12... | collective-permute-start | bytes 24584 | tf_op jit(solution)/shard_map/ppermute | solution.py:167
  48.3 4.0 %collective-permute-start.1 = (bf16[2,16,128]{2,1,0:T(8,128)(2,1)S(1)}, bf16[2,16,128]{2,1,0:T(8,128)(2,1)S(1)}, u32[]{:S(2)}, u32[]{:S(2)}) collective-permute-start(bf16[2,16,128]{2,1,0:T(8,128)(2,1)S(1)} %bitcast.52), channel_id=1, source_target_pairs={{0,4},{2,6},{4,0},{6,2},{1,5},{3,7},{5,1},{7,3},{8,12},{10,14},{12... | collective-permute-start | bytes 24584 | tf_op jit(solution)/shard_map/ppermute | solution.py:167
  52.3 3.1 %collective-permute-start.2 = (bf16[2,16,128]{2,1,0:T(8,128)(2,1)S(1)}, bf16[2,16,128]{2,1,0:T(8,128)(2,1)S(1)}, u32[]{:S(2)}, u32[]{:S(2)}) collective-permute-start(bf16[2,16,128]{2,1,0:T(8,128)(2,1)S(1)} %bitcast.53), channel_id=1, source_target_pairs={{0,6},{2,0},{4,2},{6,4},{1,7},{3,1},{5,3},{7,5},{8,14},{10,8},{12,... | collective-permute-start | bytes 24584 | tf_op jit(solution)/shard_map/ppermute | solution.py:167
  55.4 2.9 %collective-permute-done = bf16[2,16,128]{2,1,0:T(8,128)(2,1)S(1)} collective-permute-done((bf16[2,16,128]{2,1,0:T(8,128)(2,1)S(1)}, bf16[2,16,128]{2,1,0:T(8,128)(2,1)S(1)}, u32[]{:S(2)}, u32[]{:S(2)}) %collective-permute-start) | collective-permute-done | bytes 8224 | tf_op jit(solution)/shard_map/ppermute | solution.py:167
  58.3 2.2 %collective-permute-done.1 = bf16[2,16,128]{2,1,0:T(8,128)(2,1)S(1)} collective-permute-done((bf16[2,16,128]{2,1,0:T(8,128)(2,1)S(1)}, bf16[2,16,128]{2,1,0:T(8,128)(2,1)S(1)}, u32[]{:S(2)}, u32[]{:S(2)}) %collective-permute-start.1) | collective-permute-done | bytes 8224 | tf_op jit(solution)/shard_map/ppermute | solution.py:167
  60.7 9.5 %all-to-all-done.1 = bf16[64,13,2,128]{3,2,1,0:T(2,128)(2,1)S(1)} async-done(((bf16[64,13,2,128]{3,2,1,0:T(2,128)(2,1)}), bf16[64,13,2,128]{3,2,1,0:T(2,128)(2,1)S(1)}, u32[]{:S(2)}, u32[]{:S(2)}) %all-to-all-start.1) | async-done | bytes 426016 | tf_op jit(solution)/shard_map/all_to_all | solution.py:163
  70.2 0.7 shard_map.84
  71.0 15.4 %all_to_all.15 = bf16[16,16,128]{2,1,0:T(8,128)(2,1)S(1)} all-to-all(bf16[16,16,128]{2,1,0:T(8,128)(2,1)S(1)} %broadcast_in_dim.23), channel_id=1, replica_groups=mesh['section'=8,'x'=2,'za'=4,'zb'=4,'c'=2] {'za','zb'}, dimensions={0} | all-to-all | bytes 131072 | tf_op jit(solution)/shard_map/all_to_all | solution.py:30
  86.4 7.8 %all-gather.2 = bf16[64,16,128]{2,1,0:T(8,128)(2,1)S(1)} all-gather(bf16[16,16,128]{2,1,0:T(8,128)(2,1)S(1)} %all_to_all.15), channel_id=4, replica_groups=mesh['section'=8,'x'=2,'za'=4,'zb'=4,'c'=2] {'x','c'}, dimensions={0}, use_global_device_ids=true | all-gather | bytes 327680 | tf_op jit(solution)/shard_map/all_gather | solution.py:31
  94.8 3.2 %collective-permute-start.3 = (bf16[16,128]{1,0:T(8,128)(2,1)S(1)}, bf16[16,128]{1,0:T(8,128)(2,1)S(1)}, u32[]{:S(2)}, u32[]{:S(2)}) collective-permute-start(bf16[16,128]{1,0:T(8,128)(2,1)S(1)} %shard_map.85), channel_id=1, source_target_pairs={{0,64},{64,128},{128,192},{192,256},{256,320},{320,384},{384,448},... | collective-permute-start | bytes 12296 | tf_op jit(solution)/shard_map/ppermute | solution.py:233
  98.0 4.8 %collective-permute-done.3 = bf16[16,128]{1,0:T(8,128)(2,1)S(1)} collective-permute-done((bf16[16,128]{1,0:T(8,128)(2,1)S(1)}, bf16[16,128]{1,0:T(8,128)(2,1)S(1)}, u32[]{:S(2)}, u32[]{:S(2)}) %collective-permute-start.3) | collective-permute-done | bytes 4128 | tf_op jit(solution)/shard_map/ppermute | solution.py:233
  102.7 0.6 copy.17
  (41 shorter events, 2.0 us)
Async XLA Ops:
  0.0 18.2 %copy-start = (s32[1,16]{1,0:T(1,128)S(1)}, s32[1,16]{1,0:T(1,128)}, u32[]{:S(2)}) copy-start(s32[1,16]{1,0:T(1,128)} %param.14) | copy-start | bytes 196
  0.0 36.4 %copy-start.3 = (bf16[1,8192,32]{1,2,0:T(8,128)(2,1)S(1)}, bf16[1,8192,32]{1,2,0:T(8,128)(2,1)}, u32[]{:S(2)}) copy-start(bf16[1,8192,32]{1,2,0:T(8,128)(2,1)} %param.11) | copy-start | bytes 1572868
  0.0 36.4 %copy-start.4 = (bf16[1,8192]{1,0:T(2,128)(2,1)S(1)}, bf16[1,8192]{1,0:T(2,128)(2,1)}, u32[]{:S(2)}) copy-start(bf16[1,8192]{1,0:T(2,128)(2,1)} %gain_ref.1) | copy-start | bytes 49156
  1.4 27.3 %all-to-all-start = ((bf16[16,16,128]{2,1,0:T(8,128)(2,1)}), bf16[16,16,128]{2,1,0:T(8,128)(2,1)S(1)}, u32[]{:S(2)}, u32[]{:S(2)}) async-start(bf16[16,16,128]{2,1,0:T(8,128)(2,1)} %broadcast_in_dim.17), calls=%async_computation | async-start | bytes 131072 | tf_op jit(solution)/shard_map/all_to_all | solution.py:30
  19.4 23.2 %copy-start.1 = (bf16[1,8192,128]{2,1,0:T(8,128)(2,1)S(1)}, bf16[1,8192,128]{2,1,0:T(8,128)(2,1)}, u32[]{:S(2)}) copy-start(bf16[1,8192,128]{2,1,0:T(8,128)(2,1)} %param.10) | copy-start | bytes 6291460
  37.6 32.6 %all-to-all-start.1 = ((bf16[64,13,2,128]{3,2,1,0:T(2,128)(2,1)}), bf16[64,13,2,128]{3,2,1,0:T(2,128)(2,1)S(1)}, u32[]{:S(2)}, u32[]{:S(2)}) async-start(bf16[64,13,2,128]{3,2,1,0:T(2,128)(2,1)} %constant_dynamic-update-slice_fusion), calls=%async_computation.1 | async-start | bytes 851968 | tf_op jit(solution)/shard_map/all_to_all | solution.py:163
  42.5 51.8 %copy-start.5 = (bf16[1,16,128]{2,1,0:T(8,128)(2,1)S(1)}, bf16[1,16,128]{2,1,0:T(8,128)(2,1)}, u32[]{:S(2)}) copy-start(bf16[1,16,128]{2,1,0:T(8,128)(2,1)} %param.8) | copy-start | bytes 12292
  43.0 51.4 %copy-start.2 = (bf16[1,8192,128]{2,1,0:T(8,128)(2,1)S(1)}, bf16[1,8192,128]{2,1,0:T(8,128)(2,1)}, u32[]{:S(2)}) copy-start(bf16[1,8192,128]{2,1,0:T(8,128)(2,1)} %param.12) | copy-start | bytes 6291460
  45.1 13.3 %collective-permute-start = (bf16[2,16,128]{2,1,0:T(8,128)(2,1)S(1)}, bf16[2,16,128]{2,1,0:T(8,128)(2,1)S(1)}, u32[]{:S(2)}, u32[]{:S(2)}) collective-permute-start(bf16[2,16,128]{2,1,0:T(8,128)(2,1)S(1)} %bitcast.51), channel_id=1, source_target_pairs={{0,2},{2,4},{4,6},{6,0},{1,3},{3,5},{5,7},{7,1},{8,10},{10,12},{12... | collective-permute-start | bytes 24584 | tf_op jit(solution)/shard_map/ppermute | solution.py:167
  48.3 12.2 %collective-permute-start.1 = (bf16[2,16,128]{2,1,0:T(8,128)(2,1)S(1)}, bf16[2,16,128]{2,1,0:T(8,128)(2,1)S(1)}, u32[]{:S(2)}, u32[]{:S(2)}) collective-permute-start(bf16[2,16,128]{2,1,0:T(8,128)(2,1)S(1)} %bitcast.52), channel_id=1, source_target_pairs={{0,4},{2,6},{4,0},{6,2},{1,5},{3,7},{5,1},{7,3},{8,12},{10,14},{12... | collective-permute-start | bytes 24584 | tf_op jit(solution)/shard_map/ppermute | solution.py:167
  52.3 8.4 %collective-permute-start.2 = (bf16[2,16,128]{2,1,0:T(8,128)(2,1)S(1)}, bf16[2,16,128]{2,1,0:T(8,128)(2,1)S(1)}, u32[]{:S(2)}, u32[]{:S(2)}) collective-permute-start(bf16[2,16,128]{2,1,0:T(8,128)(2,1)S(1)} %bitcast.53), channel_id=1, source_target_pairs={{0,6},{2,0},{4,2},{6,4},{1,7},{3,1},{5,3},{7,5},{8,14},{10,8},{12,... | collective-permute-start | bytes 24584 | tf_op jit(solution)/shard_map/ppermute | solution.py:167
  94.8 8.0 %collective-permute-start.3 = (bf16[16,128]{1,0:T(8,128)(2,1)S(1)}, bf16[16,128]{1,0:T(8,128)(2,1)S(1)}, u32[]{:S(2)}, u32[]{:S(2)}) collective-permute-start(bf16[16,128]{1,0:T(8,128)(2,1)S(1)} %shard_map.85), channel_id=1, source_target_pairs={{0,64},{64,128},{128,192},{192,256},{256,320},{320,384},{384,448},... | collective-permute-start | bytes 12296 | tf_op jit(solution)/shard_map/ppermute | solution.py:233

commit v7 on v6

--- a/solution.py
+++ b/solution.py
@@ -53,11 +53,12 @@
         preferred_element_type=jnp.float32,
     ).astype(jnp.bfloat16)
     part = keyval.shape[1]
-    lane = lax.broadcasted_iota(jnp.int32, (part, width), 1)
-    column = lax.broadcasted_iota(jnp.int32, (part, width), 0)
-    place = jnp.where(lane == column + share_ref[0] * part, 1.0, 0.0).astype(jnp.bfloat16)
-    placed = jnp.dot(keyval, place, preferred_element_type=jnp.float32)
-    fresh_ref[...] = placed.astype(jnp.bfloat16)
+    shares = width // part
+    wide = jnp.concatenate([keyval.astype(jnp.float32)] * shares, axis=1)
+    lane = lax.broadcasted_iota(jnp.int32, (rows, width), 1)
+    first = share_ref[0] * part
+    kept = (lane >= first) & (lane < first + part)
+    fresh_ref[...] = jnp.where(kept, wide, 0.0).astype(jnp.bfloat16)
 
 
 def rotate_query(normed_ref, query_ref, cosine_ref, sine_ref, out_ref):

time: 104 us -> 104 us (level)
  no operation moved by 1% of the time
where the time goes in v7:
time: 104 us; the launch traced here: 103 us
  starting transfers between devices  33.8 us (32%)
  blocking collectives  33 us (32%)
  waiting for transfers between devices  27.3 us (26%)
  local copies, waits for them, and re-layouts  5.43 us (5%)
  Pallas kernels  2.04 us (2%)
  other arithmetic  1.4 us (1%)
    all_to_all x1, starting transfers between devices, spread(): along = lax.all_to_all(copies, LINE, 0, 0)  15.7 us
    all_gather x2, blocking collectives, spread(): full = lax.all_gather(along, ('x', 'c'))  15.5 us
    all_to_all x1, blocking collectives, spread(): along = lax.all_to_all(copies, LINE, 0, 0)  15.4 us
    ppermute x3, starting transfers between devices, body(): lax.ppermute(chip, 'zb', [(i, (i + by) % chips) for i in range(chips)])  10.3 us
    all_to_all x1, waiting for transfers between devices, body(): arrived = lax.all_to_all(sent, MINOR, 0, 0).reshape(devices, -1, HEAD_WIDTH)  9.52 us
    all_to_all x1, waiting for transfers between devices, spread(): along = lax.all_to_all(copies, LINE, 0, 0)  7.77 us
    ppermute x3, waiting for transfers between devices, body(): lax.ppermute(chip, 'zb', [(i, (i + by) % chips) for i in range(chips)])  5.27 us
    ppermute x1, waiting for transfers between devices, body(): return lax.ppermute(updated, 'section', following)[None]  4.75 us
  transfers between devices with their start and end apart: 6, of which 6 were waited for; matrix products, arithmetic and copies ran while one was open for 4% of the time, Pallas kernels for 0%

profile of v7, /device:TPU:1, one launch (start us, length us, event | category | flops | bytes accessed | tf_op | source)
XLA Modules:
  0.0 103.3 jit_solution(15396520190662095427)
XLA Ops:
  0.0 1.4 %broadcast_in_dim.17 = bf16[16,16,128]{2,1,0:T(8,128)(2,1)} broadcast(bf16[16,128]{1,0:T(8,128)(2,1)} %bitcast.44), dimensions={1,2} | broadcast | bytes 69632 | tf_op jit(solution)/shard_map/broadcast_in_dim | solution.py:29
  1.4 15.7 %all-to-all-start = ((bf16[16,16,128]{2,1,0:T(8,128)(2,1)}), bf16[16,16,128]{2,1,0:T(8,128)(2,1)S(1)}, u32[]{:S(2)}, u32[]{:S(2)}) async-start(bf16[16,16,128]{2,1,0:T(8,128)(2,1)} %broadcast_in_dim.17), calls=%async_computation | async-start | bytes 131072 | tf_op jit(solution)/shard_map/all_to_all | solution.py:30
  17.3 0.7 convert_bitcast_fusion
  18.3 1.1 %copy.14 = bf16[12,8,16,128]{3,2,1,0:T(8,128)(2,1)S(1)} copy(bf16[12,8,16,128]{3,1,2,0:T(8,128)(2,1)} %bitcast.49) | data formatting | bytes 786432
  19.7 1.1 %pad.4 = bf16[64,13,2,128]{3,2,1,0:T(2,128)(2,1)} pad(bf16[64,12,2,128]{3,2,1,0:T(2,128)(2,1)S(1)} %bitcast.46, bf16[]{:T(256)} %constant.179.clone.1), padding=0_0x0_1x0_0x0_0 | pad | bytes 819202 | tf_op jit(solution)/shard_map/jit(_pad)/pad | solution.py:126
  20.9 7.8 %all-to-all-done = bf16[16,16,128]{2,1,0:T(8,128)(2,1)S(1)} async-done(((bf16[16,16,128]{2,1,0:T(8,128)(2,1)}), bf16[16,16,128]{2,1,0:T(8,128)(2,1)S(1)}, u32[]{:S(2)}, u32[]{:S(2)}) %all-to-all-start) | async-done | bytes 65568 | tf_op jit(solution)/shard_map/all_to_all | solution.py:30
  28.7 7.7 %all-gather.gathered_ref = bf16[64,16,128]{2,1,0:T(8,128)(2,1)S(1)} all-gather(bf16[16,16,128]{2,1,0:T(8,128)(2,1)S(1)} %all-to-all-done), channel_id=2, replica_groups=mesh['section'=8,'x'=2,'za'=4,'zb'=4,'c'=2] {'x','c'}, dimensions={0}, use_global_device_ids=true | all-gather | bytes 327680 | tf_op jit(solution)/shard_map/all_gather | solution.py:31
  36.4 0.5 shard_map.82
  36.9 0.6 constant_dynamic-update-slice_fusion
  37.6 4.6 %all-to-all-start.1 = ((bf16[64,13,2,128]{3,2,1,0:T(2,128)(2,1)}), bf16[64,13,2,128]{3,2,1,0:T(2,128)(2,1)S(1)}, u32[]{:S(2)}, u32[]{:S(2)}) async-start(bf16[64,13,2,128]{3,2,1,0:T(2,128)(2,1)} %constant_dynamic-update-slice_fusion), calls=%async_computation.1 | async-start | bytes 851968 | tf_op jit(solution)/shard_map/all_to_all | solution.py:164
  42.5 0.5 shard_map.83
  43.0 2.1 %all-gather.1 = bf16[32,128]{1,0:T(8,128)(2,1)S(1)} all-gather(bf16[16,128]{1,0:T(8,128)(2,1)S(1)} %shard_map.83), channel_id=3, replica_groups=mesh['section'=8,'x'=2,'za'=4,'zb'=4,'c'=2] {'c'}, dimensions={0}, use_global_device_ids=true | all-gather | bytes 12288 | tf_op jit(solution)/shard_map/all_gather | solution.py:165
  45.0 3.2 %collective-permute-start = (bf16[2,16,128]{2,1,0:T(8,128)(2,1)S(1)}, bf16[2,16,128]{2,1,0:T(8,128)(2,1)S(1)}, u32[]{:S(2)}, u32[]{:S(2)}) collective-permute-start(bf16[2,16,128]{2,1,0:T(8,128)(2,1)S(1)} %bitcast.51), channel_id=1, source_target_pairs={{0,2},{2,4},{4,6},{6,0},{1,3},{3,5},{5,7},{7,1},{8,10},{10,12},{12... | collective-permute-start | bytes 24584 | tf_op jit(solution)/shard_map/ppermute | solution.py:168
  48.2 4.0 %collective-permute-start.1 = (bf16[2,16,128]{2,1,0:T(8,128)(2,1)S(1)}, bf16[2,16,128]{2,1,0:T(8,128)(2,1)S(1)}, u32[]{:S(2)}, u32[]{:S(2)}) collective-permute-start(bf16[2,16,128]{2,1,0:T(8,128)(2,1)S(1)} %bitcast.52), channel_id=1, source_target_pairs={{0,4},{2,6},{4,0},{6,2},{1,5},{3,7},{5,1},{7,3},{8,12},{10,14},{12... | collective-permute-start | bytes 24584 | tf_op jit(solution)/shard_map/ppermute | solution.py:168
  52.2 3.1 %collective-permute-start.2 = (bf16[2,16,128]{2,1,0:T(8,128)(2,1)S(1)}, bf16[2,16,128]{2,1,0:T(8,128)(2,1)S(1)}, u32[]{:S(2)}, u32[]{:S(2)}) collective-permute-start(bf16[2,16,128]{2,1,0:T(8,128)(2,1)S(1)} %bitcast.53), channel_id=1, source_target_pairs={{0,6},{2,0},{4,2},{6,4},{1,7},{3,1},{5,3},{7,5},{8,14},{10,8},{12,... | collective-permute-start | bytes 24584 | tf_op jit(solution)/shard_map/ppermute | solution.py:168
  55.4 2.9 %collective-permute-done = bf16[2,16,128]{2,1,0:T(8,128)(2,1)S(1)} collective-permute-done((bf16[2,16,128]{2,1,0:T(8,128)(2,1)S(1)}, bf16[2,16,128]{2,1,0:T(8,128)(2,1)S(1)}, u32[]{:S(2)}, u32[]{:S(2)}) %collective-permute-start) | collective-permute-done | bytes 8224 | tf_op jit(solution)/shard_map/ppermute | solution.py:168
  58.3 2.2 %collective-permute-done.1 = bf16[2,16,128]{2,1,0:T(8,128)(2,1)S(1)} collective-permute-done((bf16[2,16,128]{2,1,0:T(8,128)(2,1)S(1)}, bf16[2,16,128]{2,1,0:T(8,128)(2,1)S(1)}, u32[]{:S(2)}, u32[]{:S(2)}) %collective-permute-start.1) | collective-permute-done | bytes 8224 | tf_op jit(solution)/shard_map/ppermute | solution.py:168
  60.7 9.5 %all-to-all-done.1 = bf16[64,13,2,128]{3,2,1,0:T(2,128)(2,1)S(1)} async-done(((bf16[64,13,2,128]{3,2,1,0:T(2,128)(2,1)}), bf16[64,13,2,128]{3,2,1,0:T(2,128)(2,1)S(1)}, u32[]{:S(2)}, u32[]{:S(2)}) %all-to-all-start.1) | async-done | bytes 426016 | tf_op jit(solution)/shard_map/all_to_all | solution.py:164
  70.2 0.7 shard_map.84
  71.0 15.4 %all_to_all.15 = bf16[16,16,128]{2,1,0:T(8,128)(2,1)S(1)} all-to-all(bf16[16,16,128]{2,1,0:T(8,128)(2,1)S(1)} %broadcast_in_dim.23), channel_id=1, replica_groups=mesh['section'=8,'x'=2,'za'=4,'zb'=4,'c'=2] {'za','zb'}, dimensions={0} | all-to-all | bytes 131072 | tf_op jit(solution)/shard_map/all_to_all | solution.py:30
  86.4 7.8 %all-gather.2 = bf16[64,16,128]{2,1,0:T(8,128)(2,1)S(1)} all-gather(bf16[16,16,128]{2,1,0:T(8,128)(2,1)S(1)} %all_to_all.15), channel_id=4, replica_groups=mesh['section'=8,'x'=2,'za'=4,'zb'=4,'c'=2] {'x','c'}, dimensions={0}, use_global_device_ids=true | all-gather | bytes 327680 | tf_op jit(solution)/shard_map/all_gather | solution.py:31
  94.7 3.2 %collective-permute-start.3 = (bf16[16,128]{1,0:T(8,128)(2,1)S(1)}, bf16[16,128]{1,0:T(8,128)(2,1)S(1)}, u32[]{:S(2)}, u32[]{:S(2)}) collective-permute-start(bf16[16,128]{1,0:T(8,128)(2,1)S(1)} %shard_map.85), channel_id=1, source_target_pairs={{0,64},{64,128},{128,192},{192,256},{256,320},{320,384},{384,448},... | collective-permute-start | bytes 12296 | tf_op jit(solution)/shard_map/ppermute | solution.py:234
  97.9 4.8 %collective-permute-done.3 = bf16[16,128]{1,0:T(8,128)(2,1)S(1)} collective-permute-done((bf16[16,128]{1,0:T(8,128)(2,1)S(1)}, bf16[16,128]{1,0:T(8,128)(2,1)S(1)}, u32[]{:S(2)}, u32[]{:S(2)}) %collective-permute-start.3) | collective-permute-done | bytes 4128 | tf_op jit(solution)/shard_map/ppermute | solution.py:234
  102.7 0.6 copy.17
  (41 shorter events, 2.0 us)
Async XLA Ops:
  0.0 18.2 %copy-start = (s32[1,16]{1,0:T(1,128)S(1)}, s32[1,16]{1,0:T(1,128)}, u32[]{:S(2)}) copy-start(s32[1,16]{1,0:T(1,128)} %param.14) | copy-start | bytes 196
  0.0 36.4 %copy-start.3 = (bf16[1,8192,32]{1,2,0:T(8,128)(2,1)S(1)}, bf16[1,8192,32]{1,2,0:T(8,128)(2,1)}, u32[]{:S(2)}) copy-start(bf16[1,8192,32]{1,2,0:T(8,128)(2,1)} %param.11) | copy-start | bytes 1572868
  0.0 36.4 %copy-start.4 = (bf16[1,8192]{1,0:T(2,128)(2,1)S(1)}, bf16[1,8192]{1,0:T(2,128)(2,1)}, u32[]{:S(2)}) copy-start(bf16[1,8192]{1,0:T(2,128)(2,1)} %gain_ref.1) | copy-start | bytes 49156
  1.4 27.3 %all-to-all-start = ((bf16[16,16,128]{2,1,0:T(8,128)(2,1)}), bf16[16,16,128]{2,1,0:T(8,128)(2,1)S(1)}, u32[]{:S(2)}, u32[]{:S(2)}) async-start(bf16[16,16,128]{2,1,0:T(8,128)(2,1)} %broadcast_in_dim.17), calls=%async_computation | async-start | bytes 131072 | tf_op jit(solution)/shard_map/all_to_all | solution.py:30
  19.4 23.1 %copy-start.1 = (bf16[1,8192,128]{2,1,0:T(8,128)(2,1)S(1)}, bf16[1,8192,128]{2,1,0:T(8,128)(2,1)}, u32[]{:S(2)}) copy-start(bf16[1,8192,128]{2,1,0:T(8,128)(2,1)} %param.10) | copy-start | bytes 6291460
  37.6 32.6 %all-to-all-start.1 = ((bf16[64,13,2,128]{3,2,1,0:T(2,128)(2,1)}), bf16[64,13,2,128]{3,2,1,0:T(2,128)(2,1)S(1)}, u32[]{:S(2)}, u32[]{:S(2)}) async-start(bf16[64,13,2,128]{3,2,1,0:T(2,128)(2,1)} %constant_dynamic-update-slice_fusion), calls=%async_computation.1 | async-start | bytes 851968 | tf_op jit(solution)/shard_map/all_to_all | solution.py:164
  42.5 51.8 %copy-start.5 = (bf16[1,16,128]{2,1,0:T(8,128)(2,1)S(1)}, bf16[1,16,128]{2,1,0:T(8,128)(2,1)}, u32[]{:S(2)}) copy-start(bf16[1,16,128]{2,1,0:T(8,128)(2,1)} %param.8) | copy-start | bytes 12292
  43.0 51.4 %copy-start.2 = (bf16[1,8192,128]{2,1,0:T(8,128)(2,1)S(1)}, bf16[1,8192,128]{2,1,0:T(8,128)(2,1)}, u32[]{:S(2)}) copy-start(bf16[1,8192,128]{2,1,0:T(8,128)(2,1)} %param.12) | copy-start | bytes 6291460
  45.0 13.3 %collective-permute-start = (bf16[2,16,128]{2,1,0:T(8,128)(2,1)S(1)}, bf16[2,16,128]{2,1,0:T(8,128)(2,1)S(1)}, u32[]{:S(2)}, u32[]{:S(2)}) collective-permute-start(bf16[2,16,128]{2,1,0:T(8,128)(2,1)S(1)} %bitcast.51), channel_id=1, source_target_pairs={{0,2},{2,4},{4,6},{6,0},{1,3},{3,5},{5,7},{7,1},{8,10},{10,12},{12... | collective-permute-start | bytes 24584 | tf_op jit(solution)/shard_map/ppermute | solution.py:168
  48.2 12.2 %collective-permute-start.1 = (bf16[2,16,128]{2,1,0:T(8,128)(2,1)S(1)}, bf16[2,16,128]{2,1,0:T(8,128)(2,1)S(1)}, u32[]{:S(2)}, u32[]{:S(2)}) collective-permute-start(bf16[2,16,128]{2,1,0:T(8,128)(2,1)S(1)} %bitcast.52), channel_id=1, source_target_pairs={{0,4},{2,6},{4,0},{6,2},{1,5},{3,7},{5,1},{7,3},{8,12},{10,14},{12... | collective-permute-start | bytes 24584 | tf_op jit(solution)/shard_map/ppermute | solution.py:168
  52.2 8.4 %collective-permute-start.2 = (bf16[2,16,128]{2,1,0:T(8,128)(2,1)S(1)}, bf16[2,16,128]{2,1,0:T(8,128)(2,1)S(1)}, u32[]{:S(2)}, u32[]{:S(2)}) collective-permute-start(bf16[2,16,128]{2,1,0:T(8,128)(2,1)S(1)} %bitcast.53), channel_id=1, source_target_pairs={{0,6},{2,0},{4,2},{6,4},{1,7},{3,1},{5,3},{7,5},{8,14},{10,8},{12,... | collective-permute-start | bytes 24584 | tf_op jit(solution)/shard_map/ppermute | solution.py:168
  94.7 8.0 %collective-permute-start.3 = (bf16[16,128]{1,0:T(8,128)(2,1)S(1)}, bf16[16,128]{1,0:T(8,128)(2,1)S(1)}, u32[]{:S(2)}, u32[]{:S(2)}) collective-permute-start(bf16[16,128]{1,0:T(8,128)(2,1)S(1)} %shard_map.85), channel_id=1, source_target_pairs={{0,64},{64,128},{128,192},{192,256},{256,320},{320,384},{384,448},... | collective-permute-start | bytes 12296 | tf_op jit(solution)/shard_map/ppermute | solution.py:234

commit v8 on v6

--- a/solution.py
+++ b/solution.py
@@ -88,7 +88,7 @@
     weights = jnp.exp(scores - peak)
     new_weight = jnp.exp(new_score - peak)
     totals = jnp.sum(weights, axis=-1, keepdims=True) + new_weight
-    weights = pltpu.roll(weights, span, 1).astype(jnp.bfloat16)
+    weights = pltpu.roll(weights.astype(jnp.bfloat16), span, 1)
     mixture = jnp.dot(weights, entries, preferred_element_type=jnp.float32)
     mixture = mixture + new_weight * fresh_value
     out_ref[...] = (mixture / totals).astype(jnp.bfloat16)

time: 104 us -> 104 us (level)
  no operation moved by 1% of the time
where the time goes in v8:
time: 104 us; the launch traced here: 103 us
  starting transfers between devices  33.8 us (32%)
  blocking collectives  33 us (32%)
  waiting for transfers between devices  27.3 us (26%)
  local copies, waits for them, and re-layouts  5.43 us (5%)
  Pallas kernels  2.07 us (2%)
  other arithmetic  1.4 us (1%)
    all_to_all x1, starting transfers between devices, spread(): along = lax.all_to_all(copies, LINE, 0, 0)  15.7 us
    all_gather x2, blocking collectives, spread(): full = lax.all_gather(along, ('x', 'c'))  15.5 us
    all_to_all x1, blocking collectives, spread(): along = lax.all_to_all(copies, LINE, 0, 0)  15.4 us
    ppermute x3, starting transfers between devices, body(): lax.ppermute(chip, 'zb', [(i, (i + by) % chips) for i in range(chips)])  10.3 us
    all_to_all x1, waiting for transfers between devices, body(): arrived = lax.all_to_all(sent, MINOR, 0, 0).reshape(devices, -1, HEAD_WIDTH)  9.52 us
    all_to_all x1, waiting for transfers between devices, spread(): along = lax.all_to_all(copies, LINE, 0, 0)  7.77 us
    ppermute x3, waiting for transfers between devices, body(): lax.ppermute(chip, 'zb', [(i, (i + by) % chips) for i in range(chips)])  5.27 us
    ppermute x1, waiting for transfers between devices, body(): return lax.ppermute(updated, 'section', following)[None]  4.75 us
  transfers between devices with their start and end apart: 6, of which 6 were waited for; matrix products, arithmetic and copies ran while one was open for 4% of the time, Pallas kernels for 0%

profile of v8, /device:TPU:1, one launch (start us, length us, event | category | flops | bytes accessed | tf_op | source)
XLA Modules:
  0.0 103.3 jit_solution(7376764894142469362)
XLA Ops:
  0.0 1.4 %broadcast_in_dim.17 = bf16[16,16,128]{2,1,0:T(8,128)(2,1)} broadcast(bf16[16,128]{1,0:T(8,128)(2,1)} %bitcast.44), dimensions={1,2} | broadcast | bytes 69632 | tf_op jit(solution)/shard_map/broadcast_in_dim | solution.py:29
  1.4 15.7 %all-to-all-start = ((bf16[16,16,128]{2,1,0:T(8,128)(2,1)}), bf16[16,16,128]{2,1,0:T(8,128)(2,1)S(1)}, u32[]{:S(2)}, u32[]{:S(2)}) async-start(bf16[16,16,128]{2,1,0:T(8,128)(2,1)} %broadcast_in_dim.17), calls=%async_computation | async-start | bytes 131072 | tf_op jit(solution)/shard_map/all_to_all | solution.py:30
  17.3 0.7 convert_bitcast_fusion
  18.3 1.1 %copy.14 = bf16[12,8,16,128]{3,2,1,0:T(8,128)(2,1)S(1)} copy(bf16[12,8,16,128]{3,1,2,0:T(8,128)(2,1)} %bitcast.49) | data formatting | bytes 786432
  19.7 1.1 %pad.4 = bf16[64,13,2,128]{3,2,1,0:T(2,128)(2,1)} pad(bf16[64,12,2,128]{3,2,1,0:T(2,128)(2,1)S(1)} %bitcast.46, bf16[]{:T(256)} %constant.179.clone.1), padding=0_0x0_1x0_0x0_0 | pad | bytes 819202 | tf_op jit(solution)/shard_map/jit(_pad)/pad | solution.py:125
  20.9 7.8 %all-to-all-done = bf16[16,16,128]{2,1,0:T(8,128)(2,1)S(1)} async-done(((bf16[16,16,128]{2,1,0:T(8,128)(2,1)}), bf16[16,16,128]{2,1,0:T(8,128)(2,1)S(1)}, u32[]{:S(2)}, u32[]{:S(2)}) %all-to-all-start) | async-done | bytes 65568 | tf_op jit(solution)/shard_map/all_to_all | solution.py:30
  28.7 7.7 %all-gather.gathered_ref = bf16[64,16,128]{2,1,0:T(8,128)(2,1)S(1)} all-gather(bf16[16,16,128]{2,1,0:T(8,128)(2,1)S(1)} %all-to-all-done), channel_id=2, replica_groups=mesh['section'=8,'x'=2,'za'=4,'zb'=4,'c'=2] {'x','c'}, dimensions={0}, use_global_device_ids=true | all-gather | bytes 327680 | tf_op jit(solution)/shard_map/all_gather | solution.py:31
  36.4 0.5 shard_map.82
  37.0 0.6 constant_dynamic-update-slice_fusion
  37.6 4.6 %all-to-all-start.1 = ((bf16[64,13,2,128]{3,2,1,0:T(2,128)(2,1)}), bf16[64,13,2,128]{3,2,1,0:T(2,128)(2,1)S(1)}, u32[]{:S(2)}, u32[]{:S(2)}) async-start(bf16[64,13,2,128]{3,2,1,0:T(2,128)(2,1)} %constant_dynamic-update-slice_fusion), calls=%async_computation.1 | async-start | bytes 851968 | tf_op jit(solution)/shard_map/all_to_all | solution.py:163
  42.5 0.5 shard_map.83
  43.0 2.1 %all-gather.1 = bf16[32,128]{1,0:T(8,128)(2,1)S(1)} all-gather(bf16[16,128]{1,0:T(8,128)(2,1)S(1)} %shard_map.83), channel_id=3, replica_groups=mesh['section'=8,'x'=2,'za'=4,'zb'=4,'c'=2] {'c'}, dimensions={0}, use_global_device_ids=true | all-gather | bytes 12288 | tf_op jit(solution)/shard_map/all_gather | solution.py:164
  45.1 3.2 %collective-permute-start = (bf16[2,16,128]{2,1,0:T(8,128)(2,1)S(1)}, bf16[2,16,128]{2,1,0:T(8,128)(2,1)S(1)}, u32[]{:S(2)}, u32[]{:S(2)}) collective-permute-start(bf16[2,16,128]{2,1,0:T(8,128)(2,1)S(1)} %bitcast.51), channel_id=1, source_target_pairs={{0,2},{2,4},{4,6},{6,0},{1,3},{3,5},{5,7},{7,1},{8,10},{10,12},{12... | collective-permute-start | bytes 24584 | tf_op jit(solution)/shard_map/ppermute | solution.py:167
  48.3 4.0 %collective-permute-start.1 = (bf16[2,16,128]{2,1,0:T(8,128)(2,1)S(1)}, bf16[2,16,128]{2,1,0:T(8,128)(2,1)S(1)}, u32[]{:S(2)}, u32[]{:S(2)}) collective-permute-start(bf16[2,16,128]{2,1,0:T(8,128)(2,1)S(1)} %bitcast.52), channel_id=1, source_target_pairs={{0,4},{2,6},{4,0},{6,2},{1,5},{3,7},{5,1},{7,3},{8,12},{10,14},{12... | collective-permute-start | bytes 24584 | tf_op jit(solution)/shard_map/ppermute | solution.py:167
  52.3 3.1 %collective-permute-start.2 = (bf16[2,16,128]{2,1,0:T(8,128)(2,1)S(1)}, bf16[2,16,128]{2,1,0:T(8,128)(2,1)S(1)}, u32[]{:S(2)}, u32[]{:S(2)}) collective-permute-start(bf16[2,16,128]{2,1,0:T(8,128)(2,1)S(1)} %bitcast.53), channel_id=1, source_target_pairs={{0,6},{2,0},{4,2},{6,4},{1,7},{3,1},{5,3},{7,5},{8,14},{10,8},{12,... | collective-permute-start | bytes 24584 | tf_op jit(solution)/shard_map/ppermute | solution.py:167
  55.4 2.9 %collective-permute-done = bf16[2,16,128]{2,1,0:T(8,128)(2,1)S(1)} collective-permute-done((bf16[2,16,128]{2,1,0:T(8,128)(2,1)S(1)}, bf16[2,16,128]{2,1,0:T(8,128)(2,1)S(1)}, u32[]{:S(2)}, u32[]{:S(2)}) %collective-permute-start) | collective-permute-done | bytes 8224 | tf_op jit(solution)/shard_map/ppermute | solution.py:167
  58.3 2.2 %collective-permute-done.1 = bf16[2,16,128]{2,1,0:T(8,128)(2,1)S(1)} collective-permute-done((bf16[2,16,128]{2,1,0:T(8,128)(2,1)S(1)}, bf16[2,16,128]{2,1,0:T(8,128)(2,1)S(1)}, u32[]{:S(2)}, u32[]{:S(2)}) %collective-permute-start.1) | collective-permute-done | bytes 8224 | tf_op jit(solution)/shard_map/ppermute | solution.py:167
  60.7 9.5 %all-to-all-done.1 = bf16[64,13,2,128]{3,2,1,0:T(2,128)(2,1)S(1)} async-done(((bf16[64,13,2,128]{3,2,1,0:T(2,128)(2,1)}), bf16[64,13,2,128]{3,2,1,0:T(2,128)(2,1)S(1)}, u32[]{:S(2)}, u32[]{:S(2)}) %all-to-all-start.1) | async-done | bytes 426016 | tf_op jit(solution)/shard_map/all_to_all | solution.py:163
  70.2 0.7 shard_map.84
  71.0 15.4 %all_to_all.15 = bf16[16,16,128]{2,1,0:T(8,128)(2,1)S(1)} all-to-all(bf16[16,16,128]{2,1,0:T(8,128)(2,1)S(1)} %broadcast_in_dim.23), channel_id=1, replica_groups=mesh['section'=8,'x'=2,'za'=4,'zb'=4,'c'=2] {'za','zb'}, dimensions={0} | all-to-all | bytes 131072 | tf_op jit(solution)/shard_map/all_to_all | solution.py:30
  86.4 7.8 %all-gather.2 = bf16[64,16,128]{2,1,0:T(8,128)(2,1)S(1)} all-gather(bf16[16,16,128]{2,1,0:T(8,128)(2,1)S(1)} %all_to_all.15), channel_id=4, replica_groups=mesh['section'=8,'x'=2,'za'=4,'zb'=4,'c'=2] {'x','c'}, dimensions={0}, use_global_device_ids=true | all-gather | bytes 327680 | tf_op jit(solution)/shard_map/all_gather | solution.py:31
  94.7 3.2 %collective-permute-start.3 = (bf16[16,128]{1,0:T(8,128)(2,1)S(1)}, bf16[16,128]{1,0:T(8,128)(2,1)S(1)}, u32[]{:S(2)}, u32[]{:S(2)}) collective-permute-start(bf16[16,128]{1,0:T(8,128)(2,1)S(1)} %shard_map.85), channel_id=1, source_target_pairs={{0,64},{64,128},{128,192},{192,256},{256,320},{320,384},{384,448},... | collective-permute-start | bytes 12296 | tf_op jit(solution)/shard_map/ppermute | solution.py:233
  98.0 4.8 %collective-permute-done.3 = bf16[16,128]{1,0:T(8,128)(2,1)S(1)} collective-permute-done((bf16[16,128]{1,0:T(8,128)(2,1)S(1)}, bf16[16,128]{1,0:T(8,128)(2,1)S(1)}, u32[]{:S(2)}, u32[]{:S(2)}) %collective-permute-start.3) | collective-permute-done | bytes 4128 | tf_op jit(solution)/shard_map/ppermute | solution.py:233
  102.7 0.6 copy.17
  (41 shorter events, 2.0 us)
Async XLA Ops:
  0.0 18.2 %copy-start = (s32[1,16]{1,0:T(1,128)S(1)}, s32[1,16]{1,0:T(1,128)}, u32[]{:S(2)}) copy-start(s32[1,16]{1,0:T(1,128)} %param.14) | copy-start | bytes 196
  0.0 36.4 %copy-start.3 = (bf16[1,8192,32]{1,2,0:T(8,128)(2,1)S(1)}, bf16[1,8192,32]{1,2,0:T(8,128)(2,1)}, u32[]{:S(2)}) copy-start(bf16[1,8192,32]{1,2,0:T(8,128)(2,1)} %param.11) | copy-start | bytes 1572868
  0.0 36.4 %copy-start.4 = (bf16[1,8192]{1,0:T(2,128)(2,1)S(1)}, bf16[1,8192]{1,0:T(2,128)(2,1)}, u32[]{:S(2)}) copy-start(bf16[1,8192]{1,0:T(2,128)(2,1)} %gain_ref.1) | copy-start | bytes 49156
  1.4 27.3 %all-to-all-start = ((bf16[16,16,128]{2,1,0:T(8,128)(2,1)}), bf16[16,16,128]{2,1,0:T(8,128)(2,1)S(1)}, u32[]{:S(2)}, u32[]{:S(2)}) async-start(bf16[16,16,128]{2,1,0:T(8,128)(2,1)} %broadcast_in_dim.17), calls=%async_computation | async-start | bytes 131072 | tf_op jit(solution)/shard_map/all_to_all | solution.py:30
  19.4 23.2 %copy-start.1 = (bf16[1,8192,128]{2,1,0:T(8,128)(2,1)S(1)}, bf16[1,8192,128]{2,1,0:T(8,128)(2,1)}, u32[]{:S(2)}) copy-start(bf16[1,8192,128]{2,1,0:T(8,128)(2,1)} %param.10) | copy-start | bytes 6291460
  37.6 32.6 %all-to-all-start.1 = ((bf16[64,13,2,128]{3,2,1,0:T(2,128)(2,1)}), bf16[64,13,2,128]{3,2,1,0:T(2,128)(2,1)S(1)}, u32[]{:S(2)}, u32[]{:S(2)}) async-start(bf16[64,13,2,128]{3,2,1,0:T(2,128)(2,1)} %constant_dynamic-update-slice_fusion), calls=%async_computation.1 | async-start | bytes 851968 | tf_op jit(solution)/shard_map/all_to_all | solution.py:163
  42.5 51.8 %copy-start.5 = (bf16[1,16,128]{2,1,0:T(8,128)(2,1)S(1)}, bf16[1,16,128]{2,1,0:T(8,128)(2,1)}, u32[]{:S(2)}) copy-start(bf16[1,16,128]{2,1,0:T(8,128)(2,1)} %param.8) | copy-start | bytes 12292
  43.0 51.4 %copy-start.2 = (bf16[1,8192,128]{2,1,0:T(8,128)(2,1)S(1)}, bf16[1,8192,128]{2,1,0:T(8,128)(2,1)}, u32[]{:S(2)}) copy-start(bf16[1,8192,128]{2,1,0:T(8,128)(2,1)} %param.12) | copy-start | bytes 6291460
  45.1 13.3 %collective-permute-start = (bf16[2,16,128]{2,1,0:T(8,128)(2,1)S(1)}, bf16[2,16,128]{2,1,0:T(8,128)(2,1)S(1)}, u32[]{:S(2)}, u32[]{:S(2)}) collective-permute-start(bf16[2,16,128]{2,1,0:T(8,128)(2,1)S(1)} %bitcast.51), channel_id=1, source_target_pairs={{0,2},{2,4},{4,6},{6,0},{1,3},{3,5},{5,7},{7,1},{8,10},{10,12},{12... | collective-permute-start | bytes 24584 | tf_op jit(solution)/shard_map/ppermute | solution.py:167
  48.3 12.2 %collective-permute-start.1 = (bf16[2,16,128]{2,1,0:T(8,128)(2,1)S(1)}, bf16[2,16,128]{2,1,0:T(8,128)(2,1)S(1)}, u32[]{:S(2)}, u32[]{:S(2)}) collective-permute-start(bf16[2,16,128]{2,1,0:T(8,128)(2,1)S(1)} %bitcast.52), channel_id=1, source_target_pairs={{0,4},{2,6},{4,0},{6,2},{1,5},{3,7},{5,1},{7,3},{8,12},{10,14},{12... | collective-permute-start | bytes 24584 | tf_op jit(solution)/shard_map/ppermute | solution.py:167
  52.3 8.4 %collective-permute-start.2 = (bf16[2,16,128]{2,1,0:T(8,128)(2,1)S(1)}, bf16[2,16,128]{2,1,0:T(8,128)(2,1)S(1)}, u32[]{:S(2)}, u32[]{:S(2)}) collective-permute-start(bf16[2,16,128]{2,1,0:T(8,128)(2,1)S(1)} %bitcast.53), channel_id=1, source_target_pairs={{0,6},{2,0},{4,2},{6,4},{1,7},{3,1},{5,3},{7,5},{8,14},{10,8},{12,... | collective-permute-start | bytes 24584 | tf_op jit(solution)/shard_map/ppermute | solution.py:167
  94.7 8.0 %collective-permute-start.3 = (bf16[16,128]{1,0:T(8,128)(2,1)S(1)}, bf16[16,128]{1,0:T(8,128)(2,1)S(1)}, u32[]{:S(2)}, u32[]{:S(2)}) collective-permute-start(bf16[16,128]{1,0:T(8,128)(2,1)S(1)} %shard_map.85), channel_id=1, source_target_pairs={{0,64},{64,128},{128,192},{192,256},{256,320},{320,384},{384,448},... | collective-permute-start | bytes 12296 | tf_op jit(solution)/shard_map/ppermute | solution.py:233
